TPU v7x, 256 devices: a whole 4x4x8 slice. The times are simulated.
256 devices in a mesh: seq: 64 (over y, x, z_lo), head: 4 (over z_hi, core).
Axes of the slice: x: 4, y: 4, z: 8 (z_hi: 2, z_lo: 4; z = z_hi * 4 + z_lo), core: 2. Of those that a mesh axis runs over, the one named last changes fastest.
Arguments:
- layer_input: bfloat16 [1, 128, 256, 1280], P(None, 'seq'), may hold values from -16 to 16
- cotangent: bfloat16 [1, 128, 256, 1280], P(None, 'seq'), may hold values from -16 to 16
- queries: bfloat16 [1, 128, 256, 1280], P(None, None, 'seq', 'head'), may hold values from -18 to 18
- keys: bfloat16 [1, 128, 256, 1280], P(None, None, 'seq', 'head'), may hold values from -6 to 6
- values: bfloat16 [1, 128, 256, 1280], P(None, None, 'seq', 'head'), may hold values from -6 to 6
- gain: float32 [1280], replicated, may hold values from 0.25 to 1.75
- w_qkv: bfloat16 [1280, 3, 1280], P('seq', None, 'head'), may hold values from -0.15625 to 0.15625
- w_out: bfloat16 [1280, 1280], P('head', 'seq'), may hold values from -0.15625 to 0.15625
Outputs:
- branch_input_gradient: bfloat16 [1, 128, 256, 1280], P(None, 'seq', None, 'head')
- grad_wqkv: float32 [1280, 3, 1280], P('seq', None, 'head')
- grad_wout: float32 [1280, 1280], P('head', 'seq')
- gain_gradient: float32 [1280], P('head')
All inputs are finite; a program needn't handle non-finite values.
Results may differ from a plain program's by a relative error of at most 0.0064.
Values may be sent and summed in bfloat16 or wider, within the bound.
No kernel may reach another device: no remote copies, remote signals or barrier semaphores. Data moves between devices by JAX's collectives and lax.ppermute only.
A program may use at most 64 MiB of HBM per device.

v0:
```python
import jax
import jax.numpy as jnp
from jax import lax
from jax.experimental import pallas as pl
from jax.experimental.pallas import tpu as pltpu
from jax.sharding import Mesh
from jax.sharding import PartitionSpec as P

F32, BF16 = jnp.float32, jnp.bfloat16
WIDTH = 1280
HALF = WIDTH // 2
COLS = 320
PAIR = 2 * COLS
WIDE = 384
SPARE = WIDE - COLS
DH = 80
HEADS = COLS // DH
TOKENS = 512
FRAMES, PATCHES = 128, 4
SEQ = ("y", "x", "zl")
OWNED = 20
BLOCK = 4 * OWNED
EPS = 1e-06
NN, NT, TN = ((1,), (0,)), ((1,), (1,)), ((0,), (0,))
SWAP = [(0, 1), (1, 0)]
VMEM_SPEC = pl.BlockSpec(memory_space=pltpu.VMEM)
HBM_SPEC = pl.BlockSpec(memory_space=pltpu.HBM)


def dot(a, b, dims):
    return lax.dot_general(a, b, (dims, ((), ())), preferred_element_type=F32)


def one_hot(source):
    row = lax.broadcasted_iota(jnp.int32, (TOKENS, TOKENS), 0)
    col = lax.broadcasted_iota(jnp.int32, (TOKENS, TOKENS), 1)
    return jnp.where(col == source(row), 1.0, 0.0).astype(BF16)


def by_owner():
    return one_hot(lambda r: ((r >> 2) & 1) * 256 + (r >> 3) * 4 + (r & 3))


def by_patch():
    return one_hot(lambda r: (r & 3) * FRAMES + (r >> 2))


def call(kernel, out, scratch=(), vmem=60, flops=0, nbytes=0, sems=(), **specs):
    return pl.pallas_call(
        kernel,
        out_shape=[jax.ShapeDtypeStruct(shape, dtype) for shape, dtype in out],
        scratch_shapes=[pltpu.VMEM(shape, dtype) for shape, dtype in scratch]
        + [pltpu.SemaphoreType.DMA((n,)) for n in sems],
        **specs,
        compiler_params=pltpu.CompilerParams(vmem_limit_bytes=vmem * 2**20),
        cost_estimate=pl.CostEstimate(flops=flops, bytes_accessed=nbytes, transcendentals=0),
    )


def start_all(pairs, sems):
    copies = [pltpu.make_async_copy(src, dst, sems.at[i]) for i, (src, dst) in enumerate(pairs)]
    for copy in copies:
        copy.start()
    return copies


def wait_all(copies):
    for copy in copies:
        copy.wait()


def halves():
    core = lax.axis_index("core")
    mine = pl.ds(pl.multiple_of(core * HALF, 128), HALF)
    theirs = pl.ds(pl.multiple_of((1 - core) * HALF, 128), HALF)
    return mine, theirs


def pack_kernel(x_ref, cot_ref, out_ref):
    mine, _ = halves()
    order = by_owner()
    out_ref[:, :HALF] = dot(order, cot_ref[:, mine], NN).astype(BF16)
    out_ref[:, HALF:] = dot(order, x_ref[:, mine], NN).astype(BF16)


def standardized(x):
    x = x.astype(F32)
    centered = x - jnp.mean(x, axis=1, keepdims=True)
    rstd = 1.0 / jnp.sqrt(jnp.mean(centered * centered, axis=1, keepdims=True) + EPS)
    return centered * rstd, rstd


def columns(values, rows):
    lane = lax.broadcasted_iota(jnp.int32, (rows, SPARE), 1)
    out = jnp.zeros((rows, SPARE), F32)
    for i, value in enumerate(values):
        out = jnp.where(lane == i, value, out)
    return out


def split(value):
    high = value.astype(BF16).astype(F32)
    return [high, value - high]


def own_xhat_kernel(x_ref, out_ref):
    core, zh = lax.axis_index("core"), lax.axis_index("zh")
    xhat, rstd = standardized(dot(by_owner(), x_ref[...], NN))
    for h in range(4):

        @pl.when(zh * 2 + core == h)
        def _():
            out_ref[:, :COLS] = xhat[:, COLS * h : COLS * (h + 1)]

    out_ref[:, COLS:] = columns([rstd], TOKENS)


def heads_of():
    for p in range(PATCHES):
        for h in range(HEADS):
            yield p, h, slice(DH * h, DH * (h + 1)), slice(FRAMES * p, FRAMES * (p + 1))


def forward_kernel(q_ref, k_ref, v_ref, probs_ref, out_ref, p_s, o_s, t_s, sems):
    scale = DH ** (-0.5)
    for p, h, rows, lanes in heads_of():
        q, k, v = q_ref[p, rows, :], k_ref[p, rows, :], v_ref[p, rows, :]
        scores = dot(k, q, TN) * scale
        expos = jnp.exp(scores - jnp.max(scores, axis=0, keepdims=True))
        probs = expos * (1.0 / jnp.sum(expos, axis=0, keepdims=True))
        p_s[p * HEADS + h] = probs
        o_s[rows, lanes] = dot(v, probs.astype(BF16), NN).astype(BF16)
    t_s[...] = dot(by_patch(), o_s[...], NT).astype(BF16)
    wait_all(start_all([(p_s, probs_ref), (t_s, out_ref)], sems))


def main_kernel(own_ref, other_ref, q_ref, k_ref, v_ref, probs_ref, o_ref, w0_ref, w1_ref, w2_ref, w3_ref, gain_ref, *refs):
    a_ref, b_refs, pg_ref = refs[0], refs[1:5], refs[5]
    x_s, c_s, q_s, k_s, v_s, p_s, o_s, w_s, g_s, d_s, t_s, n_s, m_s, in_sems, out_sems = refs[6:]
    mine, theirs = halves()
    cots, xs = slice(0, HALF), slice(HALF, WIDTH)
    y, x = lax.axis_index("y"), lax.axis_index("x")
    c_pairs = [(own_ref.at[:, cots], c_s.at[:, mine]), (other_ref.at[:, cots], c_s.at[:, theirs])]
    for r, w_ref in enumerate((w0_ref, w1_ref, w2_ref, w3_ref)):
        for b in range(4):
            at = (y - b + 4) % 4 * 4 + (x - r + 4) % 4
            rows = pl.ds(pl.multiple_of(at * BLOCK, 16), BLOCK)
            c_pairs.append((w_ref.at[pl.ds(b * BLOCK, BLOCK)], w_s.at[rows]))
    c_in = start_all(c_pairs, in_sems.at[pl.ds(0, 18)])
    a_in = start_all([(q_ref, q_s), (k_ref, k_s), (v_ref, v_s), (probs_ref, p_s)], in_sems.at[pl.ds(18, 4)])
    x_in = start_all(
        [(own_ref.at[:, xs], x_s.at[:, mine]), (other_ref.at[:, xs], x_s.at[:, theirs]), (o_ref, o_s)],
        in_sems.at[pl.ds(22, 3)],
    )
    copies = []

    def send(pair):
        for r in range(4):
            for b in range(4):
                if pair == 0:
                    rows, to = pl.ds((b * 4 + r) * BLOCK, BLOCK), a_ref.at[r, b]
                else:
                    rows = pl.ds(pl.multiple_of(((y + r) % 4 * 4 + b) * BLOCK, 16), BLOCK)
                    to = b_refs[r].at[b]
                copy = pltpu.make_async_copy(m_s.at[pair, rows, :], to, out_sems.at[len(copies)])
                copy.start()
                copies.append(copy)

    order = by_patch()
    wait_all(c_in)
    g_tok = dot(c_s[...], w_s[...], NN).astype(BF16)
    g_s[...] = dot(g_tok, order, TN).astype(BF16)
    wait_all(a_in)
    scale = DH ** (-0.5)
    for p, h, rows, lanes in heads_of():
        q, k, v = q_s[p, rows, :], k_s[p, rows, :], v_s[p, rows, :]
        g = g_s[rows, lanes]
        probs = p_s[p * HEADS + h]
        dprobs = dot(v, g, TN)
        delta = jnp.sum(probs * dprobs, axis=0, keepdims=True)
        dscores = (probs * (dprobs - delta) * scale).astype(BF16)
        d_s[rows, lanes] = dot(k, dscores, NN).astype(BF16)
        d_s[slice(COLS + DH * h, COLS + DH * (h + 1)), lanes] = dot(q, dscores, NT).astype(BF16)
        d_s[slice(2 * COLS + DH * h, 2 * COLS + DH * (h + 1)), lanes] = dot(g, probs.astype(BF16), NT).astype(BF16)
    wait_all(x_in)
    n_s[...] = (standardized(x_s[...])[0] * gain_ref[...]).astype(BF16).T
    t_s[:, :PAIR] = dot(order, d_s[:PAIR, :], NT).astype(BF16)
    t_s[:, PAIR:] = dot(order, d_s[PAIR:, :], NT).astype(BF16)
    pg_out = start_all([(t_s, pg_ref)], out_sems.at[pl.ds(32, 1)])
    m_s[0] = dot(n_s[...], t_s[:, :PAIR], NN).astype(BF16)
    send(0)
    m_s[1, :, :COLS] = dot(n_s[...], t_s[:, PAIR:], NN).astype(BF16)
    m_s[1, :, COLS:] = dot(c_s[...], o_s[...], TN).astype(BF16)
    send(1)
    wait_all(pg_out + copies)


def norm_kernel(own_ref, other_ref, pg_ref, w_ref, gain_ref, keep_ref, send0_ref, send1_ref, x_s, p_s, w_s, h_s, sems):
    send_refs = (send0_ref, send1_ref)
    mine, theirs = halves()
    xs = slice(HALF, WIDTH)
    copies = start_all(
        [(own_ref.at[:, xs], x_s.at[:, mine]), (other_ref.at[:, xs], x_s.at[:, theirs]), (pg_ref, p_s)]
        + [(w_ref.at[:, :1024], w_s)],
        sems,
    )
    core = lax.axis_index("core")
    step = 256
    wait_all(copies[:2])
    for r in range(0, TOKENS, step):
        h_s[r : r + step, :] = standardized(x_s[r : r + step, :])[0]
    wait_all(copies[2:])
    gains = jnp.zeros((1, WIDTH), F32)
    for r in range(0, TOKENS, step):
        rows = slice(r, r + step)
        xhat = h_s[rows, :]
        grad = dot(p_s[rows, :], w_s[:, : 3 * COLS], NT)
        scaled = grad * gain_ref[...]
        gains += jnp.sum(grad * xhat, axis=0, keepdims=True)
        a = jnp.sum(scaled, axis=1, keepdims=True)
        b = jnp.sum(scaled * xhat, axis=1, keepdims=True)
        sums = columns([a, b], step)
        parts = columns(split(a) + split(b), step).astype(BF16)
        for z in range(2):
            keep_ref[z, rows, COLS:] = sums
            send_refs[z][rows, COLS:] = parts
        for c in range(2):

            @pl.when(core == c)
            def _():
                for z in range(2):
                    own, sent = 2 * z + c, 2 * z + 1 - c
                    keep_ref[z, rows, :COLS] = grad[:, COLS * own : COLS * (own + 1)]
                    send_refs[z][rows, :COLS] = grad[:, COLS * sent : COLS * (sent + 1)].astype(BF16)

    for c in range(2):

        @pl.when(core == c)
        def _():
            for z in range(2):
                own, sent = 2 * z + c, 2 * z + 1 - c
                keep_ref[z, TOKENS : TOKENS + 1, :COLS] = gains[:, COLS * own : COLS * (own + 1)]
                pair = split(gains[:, COLS * sent : COLS * (sent + 1)])
                tail = jnp.concatenate(pair + [jnp.zeros((14, COLS), F32)], axis=0)
                send_refs[z][TOKENS:, :COLS] = tail.astype(BF16)


def combine_kernel(keep_ref, got0_ref, got1_ref, out_ref):
    for z, got_ref in enumerate((got0_ref, got1_ref)):
        gains = keep_ref[z, TOKENS : TOKENS + 1, :COLS]
        gains += jnp.sum(got_ref[TOKENS : TOKENS + 16, :COLS].astype(F32), axis=0, keepdims=True)
        gains = jnp.concatenate([gains[:, 40 * i : 40 * (i + 1)] for i in range(8)], axis=0)
        gains = jnp.concatenate([jnp.zeros((8, 4), F32), gains, jnp.zeros((8, SPARE - 44), F32)], axis=1)
        gains = jnp.broadcast_to(gains[None], (64, 8, SPARE))
        keep, got = keep_ref[z, :TOKENS, :], got_ref[:TOKENS, :].astype(F32)
        grad = keep[:, :COLS] + got[:, :COLS]
        a = keep[:, COLS : COLS + 1] + got[:, COLS : COLS + 1] + got[:, COLS + 1 : COLS + 2]
        b = keep[:, COLS + 1 : COLS + 2] + got[:, COLS + 2 : COLS + 3] + got[:, COLS + 3 : COLS + 4]
        side = columns(split(a) + split(b), TOKENS).reshape(64, 8, SPARE) + gains
        out_ref[:, z, :, :COLS] = grad.reshape(64, 8, COLS).astype(BF16)
        out_ref[:, z, :, COLS:] = side.astype(BF16)


def layer_norm_kernel(got_ref, xh_ref, gain_ref, out_ref, gain_out_ref):
    head = lax.axis_index("zh") * 2 + lax.axis_index("core")
    got = (got_ref[:, 0].astype(F32) + got_ref[:, 1].astype(F32)).reshape(TOKENS, WIDE)
    a = got[:, COLS : COLS + 1] + got[:, COLS + 1 : COLS + 2]
    b = got[:, COLS + 2 : COLS + 3] + got[:, COLS + 3 : COLS + 4]
    xhat = xh_ref[:, :COLS]
    rstd = xh_ref[:, COLS : COLS + 1]
    scaled = got[:, :COLS] * gain_ref[pl.ds(head, 1), :]
    result = rstd * (scaled - a * (1.0 / WIDTH) - xhat * (b * (1.0 / WIDTH)))
    turned = dot(result.astype(BF16), by_owner(), TN).astype(BF16)
    for f in range(2):
        out_ref[f] = turned[:, 256 * f : 256 * (f + 1)]
    gains = jnp.sum(got[:, COLS:].reshape(64, 8, SPARE), axis=0)
    gain_out_ref[...] = jnp.concatenate([gains[i : i + 1, 4:44] for i in range(8)], axis=1)[0]


def add(refs):
    out = refs[0][...].astype(F32)
    for ref in refs[1:]:
        out += ref[...].astype(F32)
    return out


def sum_first_kernel(a_ref, b0_ref, b1_ref, b2_ref, b3_ref, *refs):
    a_keep, a_send, b_keep, b_send = refs[0], refs[1:4], refs[4], refs[5:8]
    i_s, a_s, b_s, sems = refs[8:]
    sources = [a_ref.at[i] for i in range(4)] + [b0_ref, b1_ref, b2_ref, b3_ref]
    copies = start_all([(source, i_s.at[i]) for i, source in enumerate(sources)], sems)
    for half, out in ((0, a_s), (4, b_s)):
        wait_all(copies[half : half + 4])
        for i in range(4):
            out[i] = add([i_s.at[half + r, i] for r in range(4)])
    y, x = lax.axis_index("y"), lax.axis_index("x")
    a_keep[...] = a_s[y]
    b_keep[...] = b_s[x]
    for r in range(3):
        a_send[r][...] = a_s[(y + r + 1) % 4].astype(BF16)
        b_send[r][...] = b_s[(x + r + 1) % 4].astype(BF16)


def sum_second_kernel(*refs):
    keep, send, s = refs[8], refs[9:12], refs[12]
    for i in range(2):
        part = add(refs[4 * i : 4 * i + 4])
        for z in range(4):
            s[z, :, PAIR * i : PAIR * (i + 1)] = part[OWNED * z : OWNED * (z + 1), :]
    z = lax.axis_index("zl")
    keep[...] = s[z]
    for r in range(3):
        send[r][...] = s[(z + r + 1) % 4].astype(BF16)


def sum_third_kernel(*refs):
    out = add(refs[:4])
    for j in range(3):
        refs[4][j] = out[:, COLS * j : COLS * (j + 1)]
    refs[5][...] = out[:, 3 * COLS :]


def shifts(axis, parts):
    return [lax.ppermute(part, axis, [(i, (i + r + 1) % 4) for i in range(4)]) for r, part in enumerate(parts)]


def line_gather(part, axis, at):
    parts = jnp.stack([part] + shifts(axis, [part] * 3))
    me = lax.axis_index(axis)
    return jnp.stack([lax.dynamic_index_in_dim(parts, (me - src) % 4, 0, False) for src in range(4)], axis=at)


def on_device(layer_input, cotangent, queries, keys, values, gain, w_qkv, w_out):
    x = layer_input.reshape(TOKENS, WIDTH)
    shard = jnp.concatenate([w_qkv.reshape(OWNED, 3 * COLS), w_out.T], axis=1)
    block = line_gather(shard, "zl", 0).reshape(BLOCK, WIDTH)
    (packed,) = call(pack_kernel, [((TOKENS, WIDTH), BF16)], flops=10**9, nbytes=4 * 2**20)(
        x, cotangent.reshape(TOKENS, WIDTH)
    )
    packed, block = lax.optimization_barrier((packed, block))
    w = lax.all_gather(block, ("y", "x")).reshape(WIDTH, WIDTH)
    own = lax.all_to_all(packed.reshape(64, 8, WIDTH), SEQ, 0, 0).reshape(TOKENS, WIDTH)
    wo = [block[:, 3 * COLS :]]
    wo = [jnp.concatenate(wo + shifts("y", wo * 3), axis=0)]
    wo += shifts("x", wo * 3)

    def turned(a):
        return a.reshape(FRAMES, PATCHES, COLS).transpose(1, 2, 0)

    q, k, v = turned(queries), turned(keys), turned(values)
    probs, o = call(
        forward_kernel,
        [((PATCHES * HEADS, FRAMES, FRAMES), F32), ((TOKENS, COLS), BF16)],
        [((PATCHES * HEADS, FRAMES, FRAMES), F32), ((COLS, TOKENS), BF16), ((TOKENS, COLS), BF16)],
        flops=2 * 10**9,
        nbytes=4 * 2**20,
        sems=[2],
        out_specs=[HBM_SPEC] * 2,
    )(q, k, v)
    (xh,) = call(own_xhat_kernel, [((TOKENS, WIDE), F32)], flops=10**9, nbytes=4 * 2**20)(x)
    gain_row = gain.reshape(1, WIDTH)
    own, wo, probs, o, xh, gain_row = lax.optimization_barrier((own, wo, probs, o, xh, gain_row))
    other = lax.ppermute(own, "core", SWAP)
    piece = ((4, BLOCK, PAIR), BF16)
    turned_shape = ((PATCHES, COLS, FRAMES), BF16)
    for_x, *for_y, pg = call(
        main_kernel,
        [((4, 4, BLOCK, PAIR), BF16)] + [piece] * 4 + [((TOKENS, 3 * COLS), BF16)],
        [
            ((TOKENS, WIDTH), BF16),
            ((TOKENS, WIDTH), BF16),
            turned_shape,
            turned_shape,
            turned_shape,
            ((PATCHES * HEADS, FRAMES, FRAMES), F32),
            ((TOKENS, COLS), BF16),
            ((WIDTH, COLS), BF16),
            ((COLS, TOKENS), BF16),
            ((3 * COLS, TOKENS), BF16),
            ((TOKENS, 3 * COLS), BF16),
            ((WIDTH, TOKENS), BF16),
            ((2, WIDTH, PAIR), BF16),
        ],
        flops=5 * 10**9,
        nbytes=12 * 2**20,
        sems=[25, 33],
        in_specs=[HBM_SPEC] * 11 + [VMEM_SPEC],
        out_specs=[HBM_SPEC] * 6,
    )(own, other, q, k, v, probs, o, *wo, gain_row)
    got_a = lax.all_to_all(for_x, "x", 0, 0)
    got_b = shifts("y", for_y[1:])
    keep, *send = call(
        norm_kernel,
        [((2, TOKENS + 8, WIDE), F32), ((TOKENS + 16, WIDE), BF16), ((TOKENS + 16, WIDE), BF16)],
        [
            ((TOKENS, WIDTH), BF16),
            ((TOKENS, 3 * COLS), BF16),
            ((WIDTH, 1024), BF16),
            ((TOKENS, WIDTH), F32),
        ],
        flops=10**9,
        nbytes=10 * 2**20,
        sems=[4],
        in_specs=[HBM_SPEC] * 4 + [VMEM_SPEC],
    )(own, other, pg, w, gain_row)
    send, got_b[0] = lax.optimization_barrier((send, got_b[0]))
    got = [lax.ppermute(part, "core", SWAP) for part in send]
    (mixed,) = call(combine_kernel, [((64, 2, 8, WIDE), BF16)], nbytes=2**20, vmem=16)(keep, *got)
    mixed, got_b = lax.optimization_barrier((mixed, got_b))
    small, wide = ((BLOCK, PAIR), BF16), ((BLOCK, PAIR), F32)
    firsts = call(
        sum_first_kernel,
        [wide, small, small, small] * 2,
        [((8, 4, BLOCK, PAIR), BF16)] + [((4, BLOCK, PAIR), F32)] * 2,
        nbytes=2**10,
        sems=[8],
        in_specs=[HBM_SPEC] * 5,
    )(got_a, for_y[0], *got_b)
    a_keep, a1, a2, a3, b_keep, b1, b2, b3 = firsts
    result = lax.all_to_all(mixed.reshape(128, 8, WIDE), SEQ + ("zh",), 0, 0)
    got_a = shifts("y", [a1, a2, a3])
    got_b = shifts("x", [b1, b2, b3])
    small, wide = ((OWNED, WIDTH), BF16), ((OWNED, WIDTH), F32)
    keep, *parts = call(sum_second_kernel, [wide, small, small, small], [((4, OWNED, WIDTH), F32)], nbytes=2**20, vmem=8)(
        a_keep, *got_a, b_keep, *got_b
    )
    grad_qkv, grad_out = call(sum_third_kernel, [((3, OWNED, COLS), F32), ((OWNED, COLS), F32)], nbytes=2**19, vmem=4)(
        keep, *shifts("zl", parts)
    )
    branch, gains = call(
        layer_norm_kernel, [((2, COLS, 256), BF16), ((COLS,), F32)], flops=10**8, nbytes=2 * 2**20, vmem=12
    )(result.reshape(64, 2, 8, WIDE), xh, gain.reshape(4, COLS))
    return (
        branch.transpose(0, 2, 1)[None],
        grad_qkv.transpose(1, 0, 2),
        grad_out.T,
        gains,
    )


def solution(mesh):
    mesh = Mesh(mesh.devices.reshape(4, 4, 4, 2, 2), ("y", "x", "zl", "zh", "core"))
    head = ("zh", "core")
    in_specs = (
        P(None, SEQ, None, None),
        P(None, SEQ, None, None),
        P(None, None, SEQ, head),
        P(None, None, SEQ, head),
        P(None, None, SEQ, head),
        P(),
        P(SEQ, None, head),
        P(head, SEQ),
    )
    out_specs = (P(None, SEQ, None, head), P(SEQ, None, head), P(head, SEQ), P(head))
    return jax.shard_map(on_device, mesh=mesh, in_specs=in_specs, out_specs=out_specs, check_vma=False)
```

profile of v0, /device:TPU:2, one launch (start us, length us, event | category | flops | bytes accessed | tf_op | source)
XLA Modules:
  0.0 161.3 jit_solution(13386644991212951065)
XLA Ops:
  9.0 1.9 %collective-permute-start = (bf16[20,1280]{1,0:T(8,128)(2,1)S(1)}, bf16[20,1280]{1,0:T(8,128)(2,1)S(1)}, u32[]{:S(2)}, u32[]{:S(2)}) collective-permute-start(bf16[20,1280]{1,0:T(8,128)(2,1)S(1)} %pad_maximum_fusion.3), channel_id=1, source_target_pairs={{0,4},{4,8},{8,12},{12,0},{1,5},{5,9},{9,13},{13,1},{2,6},{6,10},{... | collective-permute-start | bytes 153608 | tf_op jit(solution)/shard_map/ppermute | solution.py:324
  10.9 3.3 %collective-permute-start.1 = (bf16[20,1280]{1,0:T(8,128)(2,1)S(1)}, bf16[20,1280]{1,0:T(8,128)(2,1)S(1)}, u32[]{:S(2)}, u32[]{:S(2)}) collective-permute-start(bf16[20,1280]{1,0:T(8,128)(2,1)S(1)} %pad_maximum_fusion.3), channel_id=1, source_target_pairs={{0,8},{4,12},{8,0},{12,4},{1,9},{5,13},{9,1},{13,5},{2,10},{6,14},... | collective-permute-start | bytes 153608 | tf_op jit(solution)/shard_map/ppermute | solution.py:324
  16.0 3.8 %shard_map.111 = bf16[512,1280]{1,0:T(8,128)(2,1)} custom-call(bf16[512,1280]{1,0:T(8,128)(2,1)} %bitcast.31, bf16[512,1280]{1,0:T(8,128)(2,1)} %bitcast.30), custom_call_target="tpu_custom_call" | custom-call | flops 1000000000 | bytes 4194304 | tf_op jit(solution)/shard_map/pallas_call | solution.py:337
  20.6 9.1 %all-to-all-start = ((bf16[64,8,1280]{2,1,0:T(8,128)(2,1)}), bf16[64,8,1280]{2,1,0:T(8,128)(2,1)S(1)}, u32[]{:S(2)}, u32[]{:S(2)}) async-start(bf16[64,8,1280]{2,1,0:T(8,128)(2,1)} %bitcast.7), calls=%async_computation | async-start | bytes 2621440 | tf_op jit(solution)/shard_map/all_to_all | solution.py:342
  30.7 1.6 collective-permute-start.3
  32.2 2.9 %collective-permute-start.4 = (bf16[80,320]{1,0:T(8,128)(2,1)S(1)}, bf16[80,320]{1,0:T(8,128)(2,1)S(1)}, u32[]{:S(2)}, u32[]{:S(2)}) collective-permute-start(bf16[80,320]{1,0:T(8,128)(2,1)S(1)} %slice.3), channel_id=1, source_target_pairs={{0,128},{64,192},{128,0},{192,64},{1,129},{65,193},{129,1},{193,65... | collective-permute-start | bytes 153608 | tf_op jit(solution)/shard_map/ppermute | solution.py:324
  36.5 6.9 %collective-permute-done.3 = bf16[80,320]{1,0:T(8,128)(2,1)S(1)} collective-permute-done((bf16[80,320]{1,0:T(8,128)(2,1)S(1)}, bf16[80,320]{1,0:T(8,128)(2,1)S(1)}, u32[]{:S(2)}, u32[]{:S(2)}) %collective-permute-start.3) | collective-permute-done | bytes 51232 | tf_op jit(solution)/shard_map/ppermute | solution.py:324
  43.4 3.0 %collective-permute-done.4 = bf16[80,320]{1,0:T(8,128)(2,1)S(1)} collective-permute-done((bf16[80,320]{1,0:T(8,128)(2,1)S(1)}, bf16[80,320]{1,0:T(8,128)(2,1)S(1)}, u32[]{:S(2)}, u32[]{:S(2)}) %collective-permute-start.4) | collective-permute-done | bytes 51232 | tf_op jit(solution)/shard_map/ppermute | solution.py:324
  46.5 2.9 %collective-permute-start.6 = (bf16[320,320]{1,0:T(8,128)(2,1)S(1)}, bf16[320,320]{1,0:T(8,128)(2,1)S(1)}, u32[]{:S(2)}, u32[]{:S(2)}) collective-permute-start(bf16[320,320]{1,0:T(8,128)(2,1)S(1)} %pad_maximum_fusion.2.w0_ref), channel_id=1, source_target_pairs={{0,16},{16,32},{32,48},{48,0},{1,17},{17,33},{33,49},{49,1},{2,18}... | collective-permute-start | bytes 614408 | tf_op jit(solution)/shard_map/ppermute | solution.py:324
  49.4 2.2 %collective-permute-start.8 = (bf16[320,320]{1,0:T(8,128)(2,1)S(1)}, bf16[320,320]{1,0:T(8,128)(2,1)S(1)}, u32[]{:S(2)}, u32[]{:S(2)}) collective-permute-start(bf16[320,320]{1,0:T(8,128)(2,1)S(1)} %pad_maximum_fusion.2.w0_ref), channel_id=1, source_target_pairs={{0,48},{16,0},{32,16},{48,32},{1,49},{17,1},{33,17},{49,33},{2,50}... | collective-permute-start | bytes 614408 | tf_op jit(solution)/shard_map/ppermute | solution.py:324
  51.6 3.8 %shard_map.113.xh_ref = f32[512,384]{1,0:T(8,128)} custom-call(bf16[512,1280]{1,0:T(8,128)(2,1)} %bitcast.32), custom_call_target="tpu_custom_call" | custom-call | flops 1000000000 | bytes 4194304 | tf_op jit(solution)/shard_map/pallas_call | solution.py:360
  56.0 4.1 %shard_map.112 = (f32[16,128,128]{2,1,0:T(8,128)}, bf16[512,320]{1,0:T(8,128)(2,1)}) custom-call(bf16[4,320,128]{2,1,0:T(8,128)(2,1)} %bitcast.38, bf16[4,320,128]{2,1,0:T(8,128)(2,1)} %bitcast.40, bf16[4,320,128]{2,1,0:T(8,128)(2,1)} %bitcast.42), custom_call_target="tpu_custom_call" | custom-call | flops 2000000000 | bytes 4194304 | tf_op jit(solution)/shard_map/pallas_call | solution.py:351
  61.0 2.4 %collective-permute-done.8.w3_ref = bf16[320,320]{1,0:T(8,128)(2,1)S(1)} collective-permute-done((bf16[320,320]{1,0:T(8,128)(2,1)S(1)}, bf16[320,320]{1,0:T(8,128)(2,1)S(1)}, u32[]{:S(2)}, u32[]{:S(2)}) %collective-permute-start.8) | collective-permute-done | bytes 204832 | tf_op jit(solution)/shard_map/ppermute | solution.py:324
  63.7 3.0 %collective-permute-done.9.other_ref = bf16[512,1280]{1,0:T(8,128)(2,1)S(1)} collective-permute-done((bf16[512,1280]{1,0:T(8,128)(2,1)S(1)}, bf16[512,1280]{1,0:T(8,128)(2,1)S(1)}, u32[]{:S(2)}, u32[]{:S(2)}) %collective-permute-start.9) | collective-permute-done | bytes 1310752 | tf_op jit(solution)/shard_map/ppermute | solution.py:363
  67.9 12.4 %shard_map.114 = (bf16[4,4,80,640]{3,2,1,0:T(8,128)(2,1)}, bf16[4,80,640]{2,1,0:T(8,128)(2,1)}, bf16[4,80,640]{2,1,0:T(8,128)(2,1)}, bf16[4,80,640]{2,1,0:T(8,12...) custom-call(bf16[512,1280]{1,0:T(8,128)(2,1)} %bitcast.28, bf16[512,1280]{1,0:T(8,128)(2,1)} %copy-done.6, ...), custom_call_target="tpu_custom_call" | custom-call | flops 5000000000 | bytes 12582912 | tf_op jit(solution)/shard_map/pallas_call | solution.py:366
  80.3 4.4 %all-to-all-start.2 = ((bf16[4,4,80,640]{3,2,1,0:T(8,128)(2,1)}), bf16[4,4,80,640]{3,2,1,0:T(8,128)(2,1)S(1)}, u32[]{:S(2)}, u32[]{:S(2)}) async-start(bf16[4,4,80,640]{3,2,1,0:T(8,128)(2,1)} %get-tuple-element.74), calls=%async_computation.2 | async-start | bytes 3276800 | tf_op jit(solution)/shard_map/all_to_all | solution.py:390
  86.0 2.8 %collective-permute-start.13 = (bf16[4,80,640]{2,1,0:T(8,128)(2,1)}, bf16[4,80,640]{2,1,0:T(8,128)(2,1)S(1)}, u32[]{:S(2)}, u32[]{:S(2)}) collective-permute-start(bf16[4,80,640]{2,1,0:T(8,128)(2,1)} %get-tuple-element.69), channel_id=1, source_target_pairs={{0,128},{64,192},{128,0},{192,64},{1,129},{65,193},{129,1},{193,65... | collective-permute-start | bytes 1228808 | tf_op jit(solution)/shard_map/ppermute | solution.py:324
  90.3 7.7 %shard_map.115 = (f32[2,520,384]{2,1,0:T(8,128)}, bf16[528,384]{1,0:T(8,128)(2,1)}, bf16[528,384]{1,0:T(8,128)(2,1)}) custom-call(bf16[512,1280]{1,0:T(8,128)(2,1)} %bitcast.29, bf16[512,1280]{1,0:T(8,128)(2,1)} %copy-done.6, bf16[512,960]{1,0:T(8,128)(2,1)} %get-tuple-element.61.pg_ref, bf16[1280,1280]{1,0:T(8,128)(2,1)} %all-gather.3.cloned.1.call-done.w_ref, ...), custom_call_target="tpu_custom_call" | custom-call | flops 1000000000 | bytes 10485760 | tf_op jit(solution)/shard_map/pallas_call | solution.py:392
  102.3 1.9 %shard_map.116 = bf16[64,2,8,384]{3,2,1,0:T(8,128)(2,1)} custom-call(f32[2,520,384]{2,1,0:T(8,128)S(1)} %copy-done, bf16[528,384]{1,0:T(8,128)(2,1)S(1)} %collective-permute-done.11.got0_ref, bf16[528,384]{1,0:T(8,128)(2,1)S(1)} %collective-permute-done.12.got1_ref), custom_call_target="tpu_custom_call" | custom-call | bytes 1048576 | tf_op jit(solution)/shard_map/pallas_call | solution.py:408
  104.3 2.7 %collective-permute-done.13.b2_ref = bf16[4,80,640]{2,1,0:T(8,128)(2,1)S(1)} collective-permute-done((bf16[4,80,640]{2,1,0:T(8,128)(2,1)}, bf16[4,80,640]{2,1,0:T(8,128)(2,1)S(1)}, u32[]{:S(2)}, u32[]{:S(2)}) %collective-permute-start.13) | collective-permute-done | bytes 409632 | tf_op jit(solution)/shard_map/ppermute | solution.py:324
  107.8 13.6 %all-to-all-start.1 = ((bf16[128,8,384]{2,1,0:T(8,128)(2,1)}), bf16[128,8,384]{2,1,0:T(8,128)(2,1)S(1)}, u32[]{:S(2)}, u32[]{:S(2)}) async-start(bf16[128,8,384]{2,1,0:T(8,128)(2,1)} %bitcast.18), calls=%async_computation.1 | async-start | bytes 1572864 | tf_op jit(solution)/shard_map/all_to_all | solution.py:420
  121.4 3.1 %shard_map.118 = (f32[80,640]{1,0:T(8,128)}, bf16[80,640]{1,0:T(8,128)(2,1)}, bf16[80,640]{1,0:T(8,128)(2,1)}, bf16[80,640]{1,0:T(8,128)(2,1)}, f32[80,640]{1,0:...) custom-call(bf16[4,4,80,640]{3,2,1,0:T(8,128)(2,1)} %copy-done.4, ...), custom_call_target="tpu_custom_call" | custom-call | bytes 1024 | tf_op jit(solution)/shard_map/pallas_call | solution.py:411
  124.5 1.7 %collective-permute-start.15 = (bf16[80,640]{1,0:T(8,128)(2,1)}, bf16[80,640]{1,0:T(8,128)(2,1)S(1)}, u32[]{:S(2)}, u32[]{:S(2)}) collective-permute-start(bf16[80,640]{1,0:T(8,128)(2,1)} %get-tuple-element.80), channel_id=1, source_target_pairs={{0,64},{64,128},{128,192},{192,0},{1,65},{65,129},{129,193},{193,1... | collective-permute-start | bytes 307208 | tf_op jit(solution)/shard_map/ppermute | solution.py:324
  126.2 3.1 %collective-permute-start.16 = (bf16[80,640]{1,0:T(8,128)(2,1)}, bf16[80,640]{1,0:T(8,128)(2,1)S(1)}, u32[]{:S(2)}, u32[]{:S(2)}) collective-permute-start(bf16[80,640]{1,0:T(8,128)(2,1)} %get-tuple-element.81), channel_id=1, source_target_pairs={{0,128},{64,192},{128,0},{192,64},{1,129},{65,193},{129,1},{193,65... | collective-permute-start | bytes 307208 | tf_op jit(solution)/shard_map/ppermute | solution.py:324
  130.6 1.5 collective-permute-start.18
  133.1 2.2 %collective-permute-start.20 = (bf16[80,640]{1,0:T(8,128)(2,1)}, bf16[80,640]{1,0:T(8,128)(2,1)S(1)}, u32[]{:S(2)}, u32[]{:S(2)}) collective-permute-start(bf16[80,640]{1,0:T(8,128)(2,1)} %get-tuple-element.86), channel_id=1, source_target_pairs={{0,48},{16,0},{32,16},{48,32},{1,49},{17,1},{33,17},{49,33},{2,50}... | collective-permute-start | bytes 307208 | tf_op jit(solution)/shard_map/ppermute | solution.py:324
  135.4 2.2 %collective-permute-done.16.refs_2_ = bf16[80,640]{1,0:T(8,128)(2,1)S(1)} collective-permute-done((bf16[80,640]{1,0:T(8,128)(2,1)}, bf16[80,640]{1,0:T(8,128)(2,1)S(1)}, u32[]{:S(2)}, u32[]{:S(2)}) %collective-permute-start.16) | collective-permute-done | bytes 102432 | tf_op jit(solution)/shard_map/ppermute | solution.py:324
  137.6 2.8 %collective-permute-done.19.refs_6_ = bf16[80,640]{1,0:T(8,128)(2,1)S(1)} collective-permute-done((bf16[80,640]{1,0:T(8,128)(2,1)}, bf16[80,640]{1,0:T(8,128)(2,1)S(1)}, u32[]{:S(2)}, u32[]{:S(2)}) %collective-permute-start.19) | collective-permute-done | bytes 102432 | tf_op jit(solution)/shard_map/ppermute | solution.py:324
  144.5 2.8 %collective-permute-start.22 = (bf16[20,1280]{1,0:T(8,128)(2,1)S(1)}, bf16[20,1280]{1,0:T(8,128)(2,1)S(1)}, u32[]{:S(2)}, u32[]{:S(2)}) collective-permute-start(bf16[20,1280]{1,0:T(8,128)(2,1)S(1)} %get-tuple-element.89), channel_id=1, source_target_pairs={{0,8},{4,12},{8,0},{12,4},{1,9},{5,13},{9,1},{13,5},{2,10},{6,14},... | collective-permute-start | bytes 153608 | tf_op jit(solution)/shard_map/ppermute | solution.py:324
  147.3 1.7 %collective-permute-start.23 = (bf16[20,1280]{1,0:T(8,128)(2,1)S(1)}, bf16[20,1280]{1,0:T(8,128)(2,1)S(1)}, u32[]{:S(2)}, u32[]{:S(2)}) collective-permute-start(bf16[20,1280]{1,0:T(8,128)(2,1)S(1)} %get-tuple-element.90), channel_id=1, source_target_pairs={{0,12},{4,0},{8,4},{12,8},{1,13},{5,1},{9,5},{13,9},{2,14},{6,2},{... | collective-permute-start | bytes 153608 | tf_op jit(solution)/shard_map/ppermute | solution.py:324
  150.1 2.1 %collective-permute-done.22.refs_2_ = bf16[20,1280]{1,0:T(8,128)(2,1)S(1)} collective-permute-done((bf16[20,1280]{1,0:T(8,128)(2,1)S(1)}, bf16[20,1280]{1,0:T(8,128)(2,1)S(1)}, u32[]{:S(2)}, u32[]{:S(2)}) %collective-permute-start.22) | collective-permute-done | bytes 51232 | tf_op jit(solution)/shard_map/ppermute | solution.py:324
  152.9 1.6 shard_map.117
  (77 shorter events, 25.9 us)
Async XLA Ops:
  7.2 83.1 %all-gather.3.cloned.1.call-start = ((), (), s32[]{:S(2)}) async-start(), calls=%async_computation.3 | async-start | bytes 3481600 | tf_op jit(solution)/shard_map/all_gather | solution.py:341
  9.0 10.8 %collective-permute-start = (bf16[20,1280]{1,0:T(8,128)(2,1)S(1)}, bf16[20,1280]{1,0:T(8,128)(2,1)S(1)}, u32[]{:S(2)}, u32[]{:S(2)}) collective-permute-start(bf16[20,1280]{1,0:T(8,128)(2,1)S(1)} %pad_maximum_fusion.3), channel_id=1, source_target_pairs={{0,4},{4,8},{8,12},{12,0},{1,5},{5,9},{9,13},{13,1},{2,6},{6,10},{... | collective-permute-start | bytes 153608 | tf_op jit(solution)/shard_map/ppermute | solution.py:324
  10.9 8.9 %collective-permute-start.1 = (bf16[20,1280]{1,0:T(8,128)(2,1)S(1)}, bf16[20,1280]{1,0:T(8,128)(2,1)S(1)}, u32[]{:S(2)}, u32[]{:S(2)}) collective-permute-start(bf16[20,1280]{1,0:T(8,128)(2,1)S(1)} %pad_maximum_fusion.3), channel_id=1, source_target_pairs={{0,8},{4,12},{8,0},{12,4},{1,9},{5,13},{9,1},{13,5},{2,10},{6,14},... | collective-permute-start | bytes 153608 | tf_op jit(solution)/shard_map/ppermute | solution.py:324
  14.2 5.6 %collective-permute-start.2 = (bf16[20,1280]{1,0:T(8,128)(2,1)S(1)}, bf16[20,1280]{1,0:T(8,128)(2,1)S(1)}, u32[]{:S(2)}, u32[]{:S(2)}) collective-permute-start(bf16[20,1280]{1,0:T(8,128)(2,1)S(1)} %pad_maximum_fusion.3), channel_id=1, source_target_pairs={{0,12},{4,0},{8,4},{12,8},{1,13},{5,1},{9,5},{13,9},{2,14},{6,2},{... | collective-permute-start | bytes 153608 | tf_op jit(solution)/shard_map/ppermute | solution.py:324
  20.6 42.8 %all-to-all-start = ((bf16[64,8,1280]{2,1,0:T(8,128)(2,1)}), bf16[64,8,1280]{2,1,0:T(8,128)(2,1)S(1)}, u32[]{:S(2)}, u32[]{:S(2)}) async-start(bf16[64,8,1280]{2,1,0:T(8,128)(2,1)} %bitcast.7), calls=%async_computation | async-start | bytes 2621440 | tf_op jit(solution)/shard_map/all_to_all | solution.py:342
  30.7 12.7 %collective-permute-start.3 = (bf16[80,320]{1,0:T(8,128)(2,1)S(1)}, bf16[80,320]{1,0:T(8,128)(2,1)S(1)}, u32[]{:S(2)}, u32[]{:S(2)}) collective-permute-start(bf16[80,320]{1,0:T(8,128)(2,1)S(1)} %slice.3), channel_id=1, source_target_pairs={{0,64},{64,128},{128,192},{192,0},{1,65},{65,129},{129,193},{193,1... | collective-permute-start | bytes 153608 | tf_op jit(solution)/shard_map/ppermute | solution.py:324
  32.2 14.2 %collective-permute-start.4 = (bf16[80,320]{1,0:T(8,128)(2,1)S(1)}, bf16[80,320]{1,0:T(8,128)(2,1)S(1)}, u32[]{:S(2)}, u32[]{:S(2)}) collective-permute-start(bf16[80,320]{1,0:T(8,128)(2,1)S(1)} %slice.3), channel_id=1, source_target_pairs={{0,128},{64,192},{128,0},{192,64},{1,129},{65,193},{129,1},{193,65... | collective-permute-start | bytes 153608 | tf_op jit(solution)/shard_map/ppermute | solution.py:324
  35.1 11.3 %collective-permute-start.5 = (bf16[80,320]{1,0:T(8,128)(2,1)S(1)}, bf16[80,320]{1,0:T(8,128)(2,1)S(1)}, u32[]{:S(2)}, u32[]{:S(2)}) collective-permute-start(bf16[80,320]{1,0:T(8,128)(2,1)S(1)} %slice.3), channel_id=1, source_target_pairs={{0,192},{64,0},{128,64},{192,128},{1,193},{65,1},{129,65},{193,129... | collective-permute-start | bytes 153608 | tf_op jit(solution)/shard_map/ppermute | solution.py:324
  46.5 8.9 %copy-start.10 = (bf16[320,320]{1,0:T(8,128)(2,1)}, bf16[320,320]{1,0:T(8,128)(2,1)S(1)}, u32[]{:S(2)}) copy-start(bf16[320,320]{1,0:T(8,128)(2,1)S(1)} %pad_maximum_fusion.2.w0_ref) | copy-start | bytes 614404
  46.5 13.5 %collective-permute-start.6 = (bf16[320,320]{1,0:T(8,128)(2,1)S(1)}, bf16[320,320]{1,0:T(8,128)(2,1)S(1)}, u32[]{:S(2)}, u32[]{:S(2)}) collective-permute-start(bf16[320,320]{1,0:T(8,128)(2,1)S(1)} %pad_maximum_fusion.2.w0_ref), channel_id=1, source_target_pairs={{0,16},{16,32},{32,48},{48,0},{1,17},{17,33},{33,49},{49,1},{2,18}... | collective-permute-start | bytes 614408 | tf_op jit(solution)/shard_map/ppermute | solution.py:324
  49.4 11.6 %collective-permute-start.7 = (bf16[320,320]{1,0:T(8,128)(2,1)S(1)}, bf16[320,320]{1,0:T(8,128)(2,1)S(1)}, u32[]{:S(2)}, u32[]{:S(2)}) collective-permute-start(bf16[320,320]{1,0:T(8,128)(2,1)S(1)} %pad_maximum_fusion.2.w0_ref), channel_id=1, source_target_pairs={{0,32},{16,48},{32,0},{48,16},{1,33},{17,49},{33,1},{49,17},{2,34}... | collective-permute-start | bytes 614408 | tf_op jit(solution)/shard_map/ppermute | solution.py:324
  49.4 14.0 %collective-permute-start.8 = (bf16[320,320]{1,0:T(8,128)(2,1)S(1)}, bf16[320,320]{1,0:T(8,128)(2,1)S(1)}, u32[]{:S(2)}, u32[]{:S(2)}) collective-permute-start(bf16[320,320]{1,0:T(8,128)(2,1)S(1)} %pad_maximum_fusion.2.w0_ref), channel_id=1, source_target_pairs={{0,48},{16,0},{32,16},{48,32},{1,49},{17,1},{33,17},{49,33},{2,50}... | collective-permute-start | bytes 614408 | tf_op jit(solution)/shard_map/ppermute | solution.py:324
  63.4 3.3 %collective-permute-start.9 = (bf16[512,1280]{1,0:T(8,128)(2,1)S(1)}, bf16[512,1280]{1,0:T(8,128)(2,1)S(1)}, u32[]{:S(2)}, u32[]{:S(2)}) collective-permute-start(bf16[512,1280]{1,0:T(8,128)(2,1)S(1)} %bitcast.27), channel_id=1, source_target_pairs={{0,1},{1,0},{2,3},{3,2},{4,5},{5,4},{6,7},{7,6},{8,9},{9,8},{10,11... | collective-permute-start | bytes 3932168 | tf_op jit(solution)/shard_map/ppermute | solution.py:363
  80.3 26.7 %all-to-all-start.2 = ((bf16[4,4,80,640]{3,2,1,0:T(8,128)(2,1)}), bf16[4,4,80,640]{3,2,1,0:T(8,128)(2,1)S(1)}, u32[]{:S(2)}, u32[]{:S(2)}) async-start(bf16[4,4,80,640]{3,2,1,0:T(8,128)(2,1)} %get-tuple-element.74), calls=%async_computation.2 | async-start | bytes 3276800 | tf_op jit(solution)/shard_map/all_to_all | solution.py:390
  84.7 13.3 %collective-permute-start.10 = (bf16[4,80,640]{2,1,0:T(8,128)(2,1)}, bf16[4,80,640]{2,1,0:T(8,128)(2,1)S(1)}, u32[]{:S(2)}, u32[]{:S(2)}) collective-permute-start(bf16[4,80,640]{2,1,0:T(8,128)(2,1)} %get-tuple-element.65), channel_id=1, source_target_pairs={{0,64},{64,128},{128,192},{192,0},{1,65},{65,129},{129,193},{193,1... | collective-permute-start | bytes 1228808 | tf_op jit(solution)/shard_map/ppermute | solution.py:324
  86.0 20.9 %collective-permute-start.13 = (bf16[4,80,640]{2,1,0:T(8,128)(2,1)}, bf16[4,80,640]{2,1,0:T(8,128)(2,1)S(1)}, u32[]{:S(2)}, u32[]{:S(2)}) collective-permute-start(bf16[4,80,640]{2,1,0:T(8,128)(2,1)} %get-tuple-element.69), channel_id=1, source_target_pairs={{0,128},{64,192},{128,0},{192,64},{1,129},{65,193},{129,1},{193,65... | collective-permute-start | bytes 1228808 | tf_op jit(solution)/shard_map/ppermute | solution.py:324
  88.8 18.2 %collective-permute-start.14 = (bf16[4,80,640]{2,1,0:T(8,128)(2,1)}, bf16[4,80,640]{2,1,0:T(8,128)(2,1)S(1)}, u32[]{:S(2)}, u32[]{:S(2)}) collective-permute-start(bf16[4,80,640]{2,1,0:T(8,128)(2,1)} %get-tuple-element.70), channel_id=1, source_target_pairs={{0,192},{64,0},{128,64},{192,128},{1,193},{65,1},{129,65},{193,129... | collective-permute-start | bytes 1228808 | tf_op jit(solution)/shard_map/ppermute | solution.py:324
  98.0 2.3 %collective-permute-start.11 = (bf16[528,384]{1,0:T(8,128)(2,1)}, bf16[528,384]{1,0:T(8,128)(2,1)S(1)}, u32[]{:S(2)}, u32[]{:S(2)}) collective-permute-start(bf16[528,384]{1,0:T(8,128)(2,1)} %get-tuple-element.66), channel_id=1, source_target_pairs={{0,1},{1,0},{2,3},{3,2},{4,5},{5,4},{6,7},{7,6},{8,9},{9,8},{10,11... | collective-permute-start | bytes 1216520 | tf_op jit(solution)/shard_map/ppermute | solution.py:407
  98.4 2.5 %collective-permute-start.12 = (bf16[528,384]{1,0:T(8,128)(2,1)}, bf16[528,384]{1,0:T(8,128)(2,1)S(1)}, u32[]{:S(2)}, u32[]{:S(2)}) collective-permute-start(bf16[528,384]{1,0:T(8,128)(2,1)} %get-tuple-element.67), channel_id=1, source_target_pairs={{0,1},{1,0},{2,3},{3,2},{4,5},{5,4},{6,7},{7,6},{8,9},{9,8},{10,11... | collective-permute-start | bytes 1216520 | tf_op jit(solution)/shard_map/ppermute | solution.py:407
  106.9 14.5 %copy-start.8 = (bf16[4,80,640]{2,1,0:T(8,128)(2,1)}, bf16[4,80,640]{2,1,0:T(8,128)(2,1)S(1)}, u32[]{:S(2)}) copy-start(bf16[4,80,640]{2,1,0:T(8,128)(2,1)S(1)} %collective-permute-done.13.b2_ref) | copy-start | bytes 1228804
  106.9 14.4 %copy-start.4 = (bf16[4,4,80,640]{3,2,1,0:T(8,128)(2,1)}, bf16[4,4,80,640]{3,2,1,0:T(8,128)(2,1)S(1)}, u32[]{:S(2)}) copy-start(bf16[4,4,80,640]{3,2,1,0:T(8,128)(2,1)S(1)} %all-to-all-done.2.a_ref) | copy-start | bytes 4915204
  107.8 45.1 %all-to-all-start.1 = ((bf16[128,8,384]{2,1,0:T(8,128)(2,1)}), bf16[128,8,384]{2,1,0:T(8,128)(2,1)S(1)}, u32[]{:S(2)}, u32[]{:S(2)}) async-start(bf16[128,8,384]{2,1,0:T(8,128)(2,1)} %bitcast.18), calls=%async_computation.1 | async-start | bytes 1572864 | tf_op jit(solution)/shard_map/all_to_all | solution.py:420
  124.5 28.4 %copy-start.1 = (f32[512,384]{1,0:T(8,128)S(1)}, f32[512,384]{1,0:T(8,128)}, u32[]{:S(2)}) copy-start(f32[512,384]{1,0:T(8,128)} %shard_map.113.xh_ref) | copy-start | bytes 2359300
  124.5 8.6 %collective-permute-start.15 = (bf16[80,640]{1,0:T(8,128)(2,1)}, bf16[80,640]{1,0:T(8,128)(2,1)S(1)}, u32[]{:S(2)}, u32[]{:S(2)}) collective-permute-start(bf16[80,640]{1,0:T(8,128)(2,1)} %get-tuple-element.80), channel_id=1, source_target_pairs={{0,64},{64,128},{128,192},{192,0},{1,65},{65,129},{129,193},{193,1... | collective-permute-start | bytes 307208 | tf_op jit(solution)/shard_map/ppermute | solution.py:324
  126.2 11.4 %collective-permute-start.16 = (bf16[80,640]{1,0:T(8,128)(2,1)}, bf16[80,640]{1,0:T(8,128)(2,1)S(1)}, u32[]{:S(2)}, u32[]{:S(2)}) collective-permute-start(bf16[80,640]{1,0:T(8,128)(2,1)} %get-tuple-element.81), channel_id=1, source_target_pairs={{0,128},{64,192},{128,0},{192,64},{1,129},{65,193},{129,1},{193,65... | collective-permute-start | bytes 307208 | tf_op jit(solution)/shard_map/ppermute | solution.py:324
  129.3 8.3 %collective-permute-start.17 = (bf16[80,640]{1,0:T(8,128)(2,1)}, bf16[80,640]{1,0:T(8,128)(2,1)S(1)}, u32[]{:S(2)}, u32[]{:S(2)}) collective-permute-start(bf16[80,640]{1,0:T(8,128)(2,1)} %get-tuple-element.82), channel_id=1, source_target_pairs={{0,192},{64,0},{128,64},{192,128},{1,193},{65,1},{129,65},{193,129... | collective-permute-start | bytes 307208 | tf_op jit(solution)/shard_map/ppermute | solution.py:324
  130.6 7.0 %collective-permute-start.18 = (bf16[80,640]{1,0:T(8,128)(2,1)}, bf16[80,640]{1,0:T(8,128)(2,1)S(1)}, u32[]{:S(2)}, u32[]{:S(2)}) collective-permute-start(bf16[80,640]{1,0:T(8,128)(2,1)} %get-tuple-element.84), channel_id=1, source_target_pairs={{0,16},{16,32},{32,48},{48,0},{1,17},{17,33},{33,49},{49,1},{2,18}... | collective-permute-start | bytes 307208 | tf_op jit(solution)/shard_map/ppermute | solution.py:324
  132.1 8.3 %collective-permute-start.19 = (bf16[80,640]{1,0:T(8,128)(2,1)}, bf16[80,640]{1,0:T(8,128)(2,1)S(1)}, u32[]{:S(2)}, u32[]{:S(2)}) collective-permute-start(bf16[80,640]{1,0:T(8,128)(2,1)} %get-tuple-element.85), channel_id=1, source_target_pairs={{0,32},{16,48},{32,0},{48,16},{1,33},{17,49},{33,1},{49,17},{2,34}... | collective-permute-start | bytes 307208 | tf_op jit(solution)/shard_map/ppermute | solution.py:324
  133.1 8.3 %collective-permute-start.20 = (bf16[80,640]{1,0:T(8,128)(2,1)}, bf16[80,640]{1,0:T(8,128)(2,1)S(1)}, u32[]{:S(2)}, u32[]{:S(2)}) collective-permute-start(bf16[80,640]{1,0:T(8,128)(2,1)} %get-tuple-element.86), channel_id=1, source_target_pairs={{0,48},{16,0},{32,16},{48,32},{1,49},{17,1},{33,17},{49,33},{2,50}... | collective-permute-start | bytes 307208 | tf_op jit(solution)/shard_map/ppermute | solution.py:324
  143.5 6.6 %collective-permute-start.21 = (bf16[20,1280]{1,0:T(8,128)(2,1)S(1)}, bf16[20,1280]{1,0:T(8,128)(2,1)S(1)}, u32[]{:S(2)}, u32[]{:S(2)}) collective-permute-start(bf16[20,1280]{1,0:T(8,128)(2,1)S(1)} %get-tuple-element.88), channel_id=1, source_target_pairs={{0,4},{4,8},{8,12},{12,0},{1,5},{5,9},{9,13},{13,1},{2,6},{6,10},{... | collective-permute-start | bytes 153608 | tf_op jit(solution)/shard_map/ppermute | solution.py:324
  144.5 7.6 %collective-permute-start.22 = (bf16[20,1280]{1,0:T(8,128)(2,1)S(1)}, bf16[20,1280]{1,0:T(8,128)(2,1)S(1)}, u32[]{:S(2)}, u32[]{:S(2)}) collective-permute-start(bf16[20,1280]{1,0:T(8,128)(2,1)S(1)} %get-tuple-element.89), channel_id=1, source_target_pairs={{0,8},{4,12},{8,0},{12,4},{1,9},{5,13},{9,1},{13,5},{2,10},{6,14},... | collective-permute-start | bytes 153608 | tf_op jit(solution)/shard_map/ppermute | solution.py:324
  147.3 4.9 %collective-permute-start.23 = (bf16[20,1280]{1,0:T(8,128)(2,1)S(1)}, bf16[20,1280]{1,0:T(8,128)(2,1)S(1)}, u32[]{:S(2)}, u32[]{:S(2)}) collective-permute-start(bf16[20,1280]{1,0:T(8,128)(2,1)S(1)} %get-tuple-element.90), channel_id=1, source_target_pairs={{0,12},{4,0},{8,4},{12,8},{1,13},{5,1},{9,5},{13,9},{2,14},{6,2},{... | collective-permute-start | bytes 153608 | tf_op jit(solution)/shard_map/ppermute | solution.py:324
  (11 other events, 39.3 us)
Sparse Core Ops, SparseCore 0:
  20.8 65.1 all-gather.2
where the time goes:
time: 162 us; the launch traced here: 161 us
  starting transfers between devices  67.3 us (42%)
  Pallas kernels  39.3 us (24%)
  waiting for transfers between devices  30.2 us (19%)
  between operations  14.3 us (9%)
  local copies, waits for them, and re-layouts  8.54 us (5%)
  other arithmetic  1.72 us (1%)
    ppermute x21, starting transfers between devices, shifts(): lax.ppermute(part, axis, [(i, (i + r + 1) % 4) for i in range(4)])  39 us
    ppermute x21, waiting for transfers between devices, shifts(): lax.ppermute(part, axis, [(i, (i + r + 1) % 4) for i in range(4)])  25.2 us
    all_to_all x1, starting transfers between devices, on_device(): result = lax.all_to_all(mixed.reshape(128, 8, WIDE), SEQ + ('zh',), 0, 0)  13.6 us
    pallas_call x1, Pallas kernels, on_device(): call(main_kernel, [((4, 4, BLOCK, PAIR), BF16)] + [piece] * 4 + [((TOKENS...  12.4 us
    all_to_all x1, starting transfers between devices, on_device(): lax.all_to_all(packed.reshape(64, 8, WIDTH), SEQ, 0, 0)  9.12 us
    pallas_call x1, Pallas kernels, on_device(): call(norm_kernel, [((2, TOKENS + 8, WIDE), F32), ((TOKENS + 16, WIDE), BF...  7.74 us
    unnamed x31, local copies, waits for them, and re-layouts  6.1 us
    all_to_all x1, starting transfers between devices, on_device(): got_a = lax.all_to_all(for_x, 'x', 0, 0)  4.42 us
  transfers between devices with their start and end apart: 28, of which 13 were waited for; matrix products, arithmetic and copies ran while one was open for 1% of the time, Pallas kernels for 23%

commit v1 on v0

--- a/solution.py
+++ b/solution.py
@@ -284,21 +284,27 @@
     return out
 
 
-def sum_first_kernel(a_ref, b0_ref, b1_ref, b2_ref, b3_ref, *refs):
-    a_keep, a_send, b_keep, b_send = refs[0], refs[1:4], refs[4], refs[5:8]
-    i_s, a_s, b_s, sems = refs[8:]
-    sources = [a_ref.at[i] for i in range(4)] + [b0_ref, b1_ref, b2_ref, b3_ref]
-    copies = start_all([(source, i_s.at[i]) for i, source in enumerate(sources)], sems)
-    for half, out in ((0, a_s), (4, b_s)):
-        wait_all(copies[half : half + 4])
+def first_sums(axis, pieces):
+    def kernel(*refs):
+        keep, send, (i_s, o_s, sems) = refs[-7], refs[-6:-3], refs[-3:]
+        sources = [refs[0].at[i] for i in range(4)] if pieces == 1 else refs[:4]
+        wait_all(start_all([(source, i_s.at[i]) for i, source in enumerate(sources)], sems))
         for i in range(4):
-            out[i] = add([i_s.at[half + r, i] for r in range(4)])
-    y, x = lax.axis_index("y"), lax.axis_index("x")
-    a_keep[...] = a_s[y]
-    b_keep[...] = b_s[x]
-    for r in range(3):
-        a_send[r][...] = a_s[(y + r + 1) % 4].astype(BF16)
-        b_send[r][...] = b_s[(x + r + 1) % 4].astype(BF16)
+            o_s[i] = add([i_s.at[r, i] for r in range(4)])
+        me = lax.axis_index(axis)
+        keep[...] = o_s[me]
+        for r in range(3):
+            send[r][...] = o_s[(me + r + 1) % 4].astype(BF16)
+
+    small, wide = ((BLOCK, PAIR), BF16), ((BLOCK, PAIR), F32)
+    return call(
+        kernel,
+        [wide, small, small, small],
+        [((4, 4, BLOCK, PAIR), BF16), ((4, BLOCK, PAIR), F32)],
+        nbytes=2**10,
+        sems=[4],
+        in_specs=[HBM_SPEC] * pieces,
+    )
 
 
 def sum_second_kernel(*refs):
@@ -406,17 +412,10 @@
     send, got_b[0] = lax.optimization_barrier((send, got_b[0]))
     got = [lax.ppermute(part, "core", SWAP) for part in send]
     (mixed,) = call(combine_kernel, [((64, 2, 8, WIDE), BF16)], nbytes=2**20, vmem=16)(keep, *got)
-    mixed, got_b = lax.optimization_barrier((mixed, got_b))
-    small, wide = ((BLOCK, PAIR), BF16), ((BLOCK, PAIR), F32)
-    firsts = call(
-        sum_first_kernel,
-        [wide, small, small, small] * 2,
-        [((8, 4, BLOCK, PAIR), BF16)] + [((4, BLOCK, PAIR), F32)] * 2,
-        nbytes=2**10,
-        sems=[8],
-        in_specs=[HBM_SPEC] * 5,
-    )(got_a, for_y[0], *got_b)
-    a_keep, a1, a2, a3, b_keep, b1, b2, b3 = firsts
+    firsts = first_sums("y", 1)(got_a)
+    mixed, got_b, firsts = lax.optimization_barrier((mixed, got_b, firsts))
+    a_keep, a1, a2, a3 = firsts
+    b_keep, b1, b2, b3 = first_sums("x", 4)(for_y[0], *got_b)
     result = lax.all_to_all(mixed.reshape(128, 8, WIDE), SEQ + ("zh",), 0, 0)
     got_a = shifts("y", [a1, a2, a3])
     got_b = shifts("x", [b1, b2, b3])

time: 162 us -> 162 us (level)
  local copies, waits for them, and re-layouts: 8.54 us -> 5.34 us
  Pallas kernels: 39.3 us -> 41.3 us
    all_to_all x1, waiting for transfers between devices: 0.01 us -> 6.44 us  [on_device(): got_a = lax.all_to_all(for_x, 'x', 0, 0)]
    ppermute x21, waiting for transfers between devices: 25.2 us -> 20.2 us  [shifts(): lax.ppermute(part, axis, [(i, (i + r + 1) % 4) for i in range(4)])]
    unnamed x31 -> x33, local copies, waits for them, and re-layouts: 6.1 us -> 2.89 us
    ppermute x2, waiting for transfers between devices: 2.02 us -> 0.01 us  [on_device(): got = [lax.ppermute(part, 'core', SWAP) for part in send]]
    pallas_call x1 -> x2, Pallas kernels: 3.1 us -> 5.11 us  [the longest x1 2.62 us: on_device(): b_keep, b1, b2, b3 = first_sums('x', 4)(for_y[0], *got_b)]
  transfers between devices with their start and end apart: 28 -> 28, of which waited for: 13 -> 12; matrix products, arithmetic and copies ran while one was open for 1% -> 2% of each run, Pallas kernels for 23% -> 25%
where the time goes in v1:
time: 162 us; the launch traced here: 160 us
  starting transfers between devices  67.5 us (42%)
  Pallas kernels  41.3 us (25%)
  waiting for transfers between devices  29.7 us (18%)
  between operations  14.3 us (9%)
  local copies, waits for them, and re-layouts  5.34 us (3%)
  other arithmetic  1.72 us (1%)
    ppermute x21, starting transfers between devices, shifts(): lax.ppermute(part, axis, [(i, (i + r + 1) % 4) for i in range(4)])  39.2 us
    ppermute x21, waiting for transfers between devices, shifts(): lax.ppermute(part, axis, [(i, (i + r + 1) % 4) for i in range(4)])  20.2 us
    all_to_all x1, starting transfers between devices, on_device(): result = lax.all_to_all(mixed.reshape(128, 8, WIDE), SEQ + ('zh',), 0, 0)  13.2 us
    pallas_call x1, Pallas kernels, on_device(): call(main_kernel, [((4, 4, BLOCK, PAIR), BF16)] + [piece] * 4 + [((TOKENS...  12.4 us
    all_to_all x1, starting transfers between devices, on_device(): lax.all_to_all(packed.reshape(64, 8, WIDTH), SEQ, 0, 0)  9.11 us
    pallas_call x1, Pallas kernels, on_device(): call(norm_kernel, [((2, TOKENS + 8, WIDE), F32), ((TOKENS + 16, WIDE), BF...  7.82 us
    all_to_all x1, waiting for transfers between devices, on_device(): got_a = lax.all_to_all(for_x, 'x', 0, 0)  6.44 us
    all_to_all x1, starting transfers between devices, on_device(): got_a = lax.all_to_all(for_x, 'x', 0, 0)  5.25 us
  transfers between devices with their start and end apart: 28, of which 12 were waited for; matrix products, arithmetic and copies ran while one was open for 2% of the time, Pallas kernels for 25%

profile of v1, /device:TPU:2, one launch (start us, length us, event | category | flops | bytes accessed | tf_op | source)
XLA Modules:
  0.0 160.0 jit_solution(6478643475689165446)
XLA Ops:
  9.0 1.9 %collective-permute-start = (bf16[20,1280]{1,0:T(8,128)(2,1)S(1)}, bf16[20,1280]{1,0:T(8,128)(2,1)S(1)}, u32[]{:S(2)}, u32[]{:S(2)}) collective-permute-start(bf16[20,1280]{1,0:T(8,128)(2,1)S(1)} %pad_maximum_fusion.3), channel_id=1, source_target_pairs={{0,4},{4,8},{8,12},{12,0},{1,5},{5,9},{9,13},{13,1},{2,6},{6,10},{... | collective-permute-start | bytes 153608 | tf_op jit(solution)/shard_map/ppermute | solution.py:330
  10.9 3.3 %collective-permute-start.1 = (bf16[20,1280]{1,0:T(8,128)(2,1)S(1)}, bf16[20,1280]{1,0:T(8,128)(2,1)S(1)}, u32[]{:S(2)}, u32[]{:S(2)}) collective-permute-start(bf16[20,1280]{1,0:T(8,128)(2,1)S(1)} %pad_maximum_fusion.3), channel_id=1, source_target_pairs={{0,8},{4,12},{8,0},{12,4},{1,9},{5,13},{9,1},{13,5},{2,10},{6,14},... | collective-permute-start | bytes 153608 | tf_op jit(solution)/shard_map/ppermute | solution.py:330
  16.0 3.8 %shard_map.111 = bf16[512,1280]{1,0:T(8,128)(2,1)} custom-call(bf16[512,1280]{1,0:T(8,128)(2,1)} %bitcast.31, bf16[512,1280]{1,0:T(8,128)(2,1)} %bitcast.30), custom_call_target="tpu_custom_call" | custom-call | flops 1000000000 | bytes 4194304 | tf_op jit(solution)/shard_map/pallas_call | solution.py:343
  20.7 9.1 %all-to-all-start = ((bf16[64,8,1280]{2,1,0:T(8,128)(2,1)}), bf16[64,8,1280]{2,1,0:T(8,128)(2,1)S(1)}, u32[]{:S(2)}, u32[]{:S(2)}) async-start(bf16[64,8,1280]{2,1,0:T(8,128)(2,1)} %bitcast.7), calls=%async_computation | async-start | bytes 2621440 | tf_op jit(solution)/shard_map/all_to_all | solution.py:348
  30.7 1.6 collective-permute-start.3
  32.2 2.9 %collective-permute-start.4 = (bf16[80,320]{1,0:T(8,128)(2,1)S(1)}, bf16[80,320]{1,0:T(8,128)(2,1)S(1)}, u32[]{:S(2)}, u32[]{:S(2)}) collective-permute-start(bf16[80,320]{1,0:T(8,128)(2,1)S(1)} %slice.3), channel_id=1, source_target_pairs={{0,128},{64,192},{128,0},{192,64},{1,129},{65,193},{129,1},{193,65... | collective-permute-start | bytes 153608 | tf_op jit(solution)/shard_map/ppermute | solution.py:330
  36.5 6.9 %collective-permute-done.3 = bf16[80,320]{1,0:T(8,128)(2,1)S(1)} collective-permute-done((bf16[80,320]{1,0:T(8,128)(2,1)S(1)}, bf16[80,320]{1,0:T(8,128)(2,1)S(1)}, u32[]{:S(2)}, u32[]{:S(2)}) %collective-permute-start.3) | collective-permute-done | bytes 51232 | tf_op jit(solution)/shard_map/ppermute | solution.py:330
  43.4 3.0 %collective-permute-done.4 = bf16[80,320]{1,0:T(8,128)(2,1)S(1)} collective-permute-done((bf16[80,320]{1,0:T(8,128)(2,1)S(1)}, bf16[80,320]{1,0:T(8,128)(2,1)S(1)}, u32[]{:S(2)}, u32[]{:S(2)}) %collective-permute-start.4) | collective-permute-done | bytes 51232 | tf_op jit(solution)/shard_map/ppermute | solution.py:330
  46.5 3.0 %collective-permute-start.6 = (bf16[320,320]{1,0:T(8,128)(2,1)S(1)}, bf16[320,320]{1,0:T(8,128)(2,1)S(1)}, u32[]{:S(2)}, u32[]{:S(2)}) collective-permute-start(bf16[320,320]{1,0:T(8,128)(2,1)S(1)} %pad_maximum_fusion.2.w0_ref), channel_id=1, source_target_pairs={{0,16},{16,32},{32,48},{48,0},{1,17},{17,33},{33,49},{49,1},{2,18}... | collective-permute-start | bytes 614408 | tf_op jit(solution)/shard_map/ppermute | solution.py:330
  49.4 2.2 %collective-permute-start.8 = (bf16[320,320]{1,0:T(8,128)(2,1)S(1)}, bf16[320,320]{1,0:T(8,128)(2,1)}, u32[]{:S(2)}, u32[]{:S(2)}) collective-permute-start(bf16[320,320]{1,0:T(8,128)(2,1)S(1)} %pad_maximum_fusion.2.w0_ref), channel_id=1, source_target_pairs={{0,48},{16,0},{32,16},{48,32},{1,49},{17,1},{33,17},{49,33},{2,50}... | collective-permute-start | bytes 614408 | tf_op jit(solution)/shard_map/ppermute | solution.py:330
  51.6 3.8 %shard_map.113.xh_ref = f32[512,384]{1,0:T(8,128)} custom-call(bf16[512,1280]{1,0:T(8,128)(2,1)} %bitcast.32), custom_call_target="tpu_custom_call" | custom-call | flops 1000000000 | bytes 4194304 | tf_op jit(solution)/shard_map/pallas_call | solution.py:366
  56.0 4.0 %shard_map.112 = (f32[16,128,128]{2,1,0:T(8,128)}, bf16[512,320]{1,0:T(8,128)(2,1)}) custom-call(bf16[4,320,128]{2,1,0:T(8,128)(2,1)} %bitcast.38, bf16[4,320,128]{2,1,0:T(8,128)(2,1)} %bitcast.40, bf16[4,320,128]{2,1,0:T(8,128)(2,1)} %bitcast.42), custom_call_target="tpu_custom_call" | custom-call | flops 2000000000 | bytes 4194304 | tf_op jit(solution)/shard_map/pallas_call | solution.py:357
  61.0 2.5 %collective-permute-done.8.w3_ref = bf16[320,320]{1,0:T(8,128)(2,1)} collective-permute-done((bf16[320,320]{1,0:T(8,128)(2,1)S(1)}, bf16[320,320]{1,0:T(8,128)(2,1)}, u32[]{:S(2)}, u32[]{:S(2)}) %collective-permute-start.8) | collective-permute-done | bytes 204832 | tf_op jit(solution)/shard_map/ppermute | solution.py:330
  63.5 3.0 %collective-permute-done.9.other_ref = bf16[512,1280]{1,0:T(8,128)(2,1)S(1)} collective-permute-done((bf16[512,1280]{1,0:T(8,128)(2,1)S(1)}, bf16[512,1280]{1,0:T(8,128)(2,1)S(1)}, u32[]{:S(2)}, u32[]{:S(2)}) %collective-permute-start.9) | collective-permute-done | bytes 1310752 | tf_op jit(solution)/shard_map/ppermute | solution.py:369
  67.6 12.4 %shard_map.114 = (bf16[4,4,80,640]{3,2,1,0:T(8,128)(2,1)}, bf16[4,80,640]{2,1,0:T(8,128)(2,1)}, bf16[4,80,640]{2,1,0:T(8,128)(2,1)}, bf16[4,80,640]{2,1,0:T(8,12...) custom-call(bf16[512,1280]{1,0:T(8,128)(2,1)} %bitcast.28, bf16[512,1280]{1,0:T(8,128)(2,1)} %copy-done.5, ...), custom_call_target="tpu_custom_call" | custom-call | flops 5000000000 | bytes 12582912 | tf_op jit(solution)/shard_map/pallas_call | solution.py:372
  80.0 5.2 %all-to-all-start.1 = ((bf16[4,4,80,640]{3,2,1,0:T(8,128)(2,1)}), bf16[4,4,80,640]{3,2,1,0:T(8,128)(2,1)}, u32[]{:S(2)}, u32[]{:S(2)}) async-start(bf16[4,4,80,640]{3,2,1,0:T(8,128)(2,1)} %get-tuple-element.75), calls=%async_computation.1 | async-start | bytes 3276800 | tf_op jit(solution)/shard_map/all_to_all | solution.py:396
  86.8 2.7 %collective-permute-start.13 = (bf16[4,80,640]{2,1,0:T(8,128)(2,1)}, bf16[4,80,640]{2,1,0:T(8,128)(2,1)S(1)}, u32[]{:S(2)}, u32[]{:S(2)}) collective-permute-start(bf16[4,80,640]{2,1,0:T(8,128)(2,1)} %get-tuple-element.73), channel_id=1, source_target_pairs={{0,128},{64,192},{128,0},{192,64},{1,129},{65,193},{129,1},{193,65... | collective-permute-start | bytes 1228808 | tf_op jit(solution)/shard_map/ppermute | solution.py:330
  90.6 7.8 %shard_map.115 = (f32[2,520,384]{2,1,0:T(8,128)}, bf16[528,384]{1,0:T(8,128)(2,1)}, bf16[528,384]{1,0:T(8,128)(2,1)}) custom-call(bf16[512,1280]{1,0:T(8,128)(2,1)} %bitcast.29, bf16[512,1280]{1,0:T(8,128)(2,1)} %copy-done.5, bf16[512,960]{1,0:T(8,128)(2,1)} %get-tuple-element.65.pg_ref, bf16[1280,1280]{1,0:T(8,128)(2,1)} %all-gather.3.cloned.1.call-done.w_ref, ...), custom_call_target="tpu_custom_call" | custom-call | flops 1000000000 | bytes 10485760 | tf_op jit(solution)/shard_map/pallas_call | solution.py:398
  99.3 6.4 %all-to-all-done.1.refs_0_ = bf16[4,4,80,640]{3,2,1,0:T(8,128)(2,1)} async-done(((bf16[4,4,80,640]{3,2,1,0:T(8,128)(2,1)}), bf16[4,4,80,640]{3,2,1,0:T(8,128)(2,1)}, u32[]{:S(2)}, u32[]{:S(2)}) %all-to-all-start.1) | async-done | bytes 1638432 | tf_op jit(solution)/shard_map/all_to_all | solution.py:396
  105.7 2.5 %shard_map.117 = (f32[80,640]{1,0:T(8,128)}, bf16[80,640]{1,0:T(8,128)(2,1)}, bf16[80,640]{1,0:T(8,128)(2,1)}, bf16[80,640]{1,0:T(8,128)(2,1)}) custom-call(bf16[4,4,80,640]{3,2,1,0:T(8,128)(2,1)} %all-to-all-done.1.refs_0_), custom_call_target="tpu_custom_call" | custom-call | bytes 1024 | tf_op jit(solution)/shard_map/pallas_call | solution.py:415
  108.3 2.0 %shard_map.116 = bf16[64,2,8,384]{3,2,1,0:T(8,128)(2,1)} custom-call(f32[2,520,384]{2,1,0:T(8,128)S(1)} %copy-done, bf16[528,384]{1,0:T(8,128)(2,1)S(1)} %collective-permute-done.11.got0_ref, bf16[528,384]{1,0:T(8,128)(2,1)S(1)} %collective-permute-done.12.got1_ref), custom_call_target="tpu_custom_call" | custom-call | bytes 1048576 | tf_op jit(solution)/shard_map/pallas_call | solution.py:414
  110.3 13.2 %all-to-all-start.2 = ((bf16[128,8,384]{2,1,0:T(8,128)(2,1)}), bf16[128,8,384]{2,1,0:T(8,128)(2,1)S(1)}, u32[]{:S(2)}, u32[]{:S(2)}) async-start(bf16[128,8,384]{2,1,0:T(8,128)(2,1)} %bitcast.18), calls=%async_computation.2 | async-start | bytes 1572864 | tf_op jit(solution)/shard_map/all_to_all | solution.py:419
  123.5 2.6 %shard_map.119 = (f32[80,640]{1,0:T(8,128)}, bf16[80,640]{1,0:T(8,128)(2,1)}, bf16[80,640]{1,0:T(8,128)(2,1)}, bf16[80,640]{1,0:T(8,128)(2,1)}) custom-call(bf16[4,80,640]{2,1,0:T(8,128)(2,1)} %get-tuple-element.87.refs_0_, bf16[4,80,640]{2,1,0:T(8,128)(2,1)} %copy-done.6, bf16[4,80,640]{2,1,0:T(8,128)(2,1)} %copy-done.7, ...), custom_call_target="tpu_custom_call" | custom-call | bytes 1024 | tf_op jit(solution)/shard_map/pallas_call | solution.py:418
  126.1 1.5 collective-permute-start.18
  129.1 1.8 %collective-permute-start.20 = (bf16[80,640]{1,0:T(8,128)(2,1)}, bf16[80,640]{1,0:T(8,128)(2,1)S(1)}, u32[]{:S(2)}, u32[]{:S(2)}) collective-permute-start(bf16[80,640]{1,0:T(8,128)(2,1)} %get-tuple-element.94), channel_id=1, source_target_pairs={{0,48},{16,0},{32,16},{48,32},{1,49},{17,1},{33,17},{49,33},{2,50}... | collective-permute-start | bytes 307208 | tf_op jit(solution)/shard_map/ppermute | solution.py:330
  130.9 1.7 %collective-permute-start.15 = (bf16[80,640]{1,0:T(8,128)(2,1)S(1)}, bf16[80,640]{1,0:T(8,128)(2,1)S(1)}, u32[]{:S(2)}, u32[]{:S(2)}) collective-permute-start(bf16[80,640]{1,0:T(8,128)(2,1)S(1)} %copy-done.15), channel_id=1, source_target_pairs={{0,64},{64,128},{128,192},{192,0},{1,65},{65,129},{129,193},{193,1... | collective-permute-start | bytes 307208 | tf_op jit(solution)/shard_map/ppermute | solution.py:330
  132.6 3.1 %collective-permute-start.16 = (bf16[80,640]{1,0:T(8,128)(2,1)S(1)}, bf16[80,640]{1,0:T(8,128)(2,1)S(1)}, u32[]{:S(2)}, u32[]{:S(2)}) collective-permute-start(bf16[80,640]{1,0:T(8,128)(2,1)S(1)} %copy-done.14), channel_id=1, source_target_pairs={{0,128},{64,192},{128,0},{192,64},{1,129},{65,193},{129,1},{193,65... | collective-permute-start | bytes 307208 | tf_op jit(solution)/shard_map/ppermute | solution.py:330
  139.5 2.3 %collective-permute-done.16.refs_2_ = bf16[80,640]{1,0:T(8,128)(2,1)S(1)} collective-permute-done((bf16[80,640]{1,0:T(8,128)(2,1)S(1)}, bf16[80,640]{1,0:T(8,128)(2,1)S(1)}, u32[]{:S(2)}, u32[]{:S(2)}) %collective-permute-start.16) | collective-permute-done | bytes 102432 | tf_op jit(solution)/shard_map/ppermute | solution.py:330
  142.9 1.6 %collective-permute-start.21 = (bf16[20,1280]{1,0:T(8,128)(2,1)S(1)}, bf16[20,1280]{1,0:T(8,128)(2,1)S(1)}, u32[]{:S(2)}, u32[]{:S(2)}) collective-permute-start(bf16[20,1280]{1,0:T(8,128)(2,1)S(1)} %get-tuple-element.96), channel_id=1, source_target_pairs={{0,4},{4,8},{8,12},{12,0},{1,5},{5,9},{9,13},{13,1},{2,6},{6,10},{... | collective-permute-start | bytes 153608 | tf_op jit(solution)/shard_map/ppermute | solution.py:330
  144.6 2.1 %collective-permute-start.22 = (bf16[20,1280]{1,0:T(8,128)(2,1)S(1)}, bf16[20,1280]{1,0:T(8,128)(2,1)S(1)}, u32[]{:S(2)}, u32[]{:S(2)}) collective-permute-start(bf16[20,1280]{1,0:T(8,128)(2,1)S(1)} %get-tuple-element.97), channel_id=1, source_target_pairs={{0,8},{4,12},{8,0},{12,4},{1,9},{5,13},{9,1},{13,5},{2,10},{6,14},... | collective-permute-start | bytes 153608 | tf_op jit(solution)/shard_map/ppermute | solution.py:330
  146.6 2.1 %collective-permute-start.23 = (bf16[20,1280]{1,0:T(8,128)(2,1)S(1)}, bf16[20,1280]{1,0:T(8,128)(2,1)S(1)}, u32[]{:S(2)}, u32[]{:S(2)}) collective-permute-start(bf16[20,1280]{1,0:T(8,128)(2,1)S(1)} %get-tuple-element.98), channel_id=1, source_target_pairs={{0,12},{4,0},{8,4},{12,8},{1,13},{5,1},{9,5},{13,9},{2,14},{6,2},{... | collective-permute-start | bytes 153608 | tf_op jit(solution)/shard_map/ppermute | solution.py:330
  151.6 1.6 shard_map.118
  (80 shorter events, 22.1 us)
Async XLA Ops:
  7.2 83.5 %all-gather.3.cloned.1.call-start = ((), (), s32[]{:S(2)}) async-start(), calls=%async_computation.3 | async-start | bytes 3481600 | tf_op jit(solution)/shard_map/all_gather | solution.py:347
  9.0 10.8 %collective-permute-start = (bf16[20,1280]{1,0:T(8,128)(2,1)S(1)}, bf16[20,1280]{1,0:T(8,128)(2,1)S(1)}, u32[]{:S(2)}, u32[]{:S(2)}) collective-permute-start(bf16[20,1280]{1,0:T(8,128)(2,1)S(1)} %pad_maximum_fusion.3), channel_id=1, source_target_pairs={{0,4},{4,8},{8,12},{12,0},{1,5},{5,9},{9,13},{13,1},{2,6},{6,10},{... | collective-permute-start | bytes 153608 | tf_op jit(solution)/shard_map/ppermute | solution.py:330
  10.9 8.9 %collective-permute-start.1 = (bf16[20,1280]{1,0:T(8,128)(2,1)S(1)}, bf16[20,1280]{1,0:T(8,128)(2,1)S(1)}, u32[]{:S(2)}, u32[]{:S(2)}) collective-permute-start(bf16[20,1280]{1,0:T(8,128)(2,1)S(1)} %pad_maximum_fusion.3), channel_id=1, source_target_pairs={{0,8},{4,12},{8,0},{12,4},{1,9},{5,13},{9,1},{13,5},{2,10},{6,14},... | collective-permute-start | bytes 153608 | tf_op jit(solution)/shard_map/ppermute | solution.py:330
  14.2 5.6 %collective-permute-start.2 = (bf16[20,1280]{1,0:T(8,128)(2,1)S(1)}, bf16[20,1280]{1,0:T(8,128)(2,1)S(1)}, u32[]{:S(2)}, u32[]{:S(2)}) collective-permute-start(bf16[20,1280]{1,0:T(8,128)(2,1)S(1)} %pad_maximum_fusion.3), channel_id=1, source_target_pairs={{0,12},{4,0},{8,4},{12,8},{1,13},{5,1},{9,5},{13,9},{2,14},{6,2},{... | collective-permute-start | bytes 153608 | tf_op jit(solution)/shard_map/ppermute | solution.py:330
  20.7 42.8 %all-to-all-start = ((bf16[64,8,1280]{2,1,0:T(8,128)(2,1)}), bf16[64,8,1280]{2,1,0:T(8,128)(2,1)S(1)}, u32[]{:S(2)}, u32[]{:S(2)}) async-start(bf16[64,8,1280]{2,1,0:T(8,128)(2,1)} %bitcast.7), calls=%async_computation | async-start | bytes 2621440 | tf_op jit(solution)/shard_map/all_to_all | solution.py:348
  30.7 12.7 %collective-permute-start.3 = (bf16[80,320]{1,0:T(8,128)(2,1)S(1)}, bf16[80,320]{1,0:T(8,128)(2,1)S(1)}, u32[]{:S(2)}, u32[]{:S(2)}) collective-permute-start(bf16[80,320]{1,0:T(8,128)(2,1)S(1)} %slice.3), channel_id=1, source_target_pairs={{0,64},{64,128},{128,192},{192,0},{1,65},{65,129},{129,193},{193,1... | collective-permute-start | bytes 153608 | tf_op jit(solution)/shard_map/ppermute | solution.py:330
  32.2 14.2 %collective-permute-start.4 = (bf16[80,320]{1,0:T(8,128)(2,1)S(1)}, bf16[80,320]{1,0:T(8,128)(2,1)S(1)}, u32[]{:S(2)}, u32[]{:S(2)}) collective-permute-start(bf16[80,320]{1,0:T(8,128)(2,1)S(1)} %slice.3), channel_id=1, source_target_pairs={{0,128},{64,192},{128,0},{192,64},{1,129},{65,193},{129,1},{193,65... | collective-permute-start | bytes 153608 | tf_op jit(solution)/shard_map/ppermute | solution.py:330
  35.1 11.3 %collective-permute-start.5 = (bf16[80,320]{1,0:T(8,128)(2,1)S(1)}, bf16[80,320]{1,0:T(8,128)(2,1)S(1)}, u32[]{:S(2)}, u32[]{:S(2)}) collective-permute-start(bf16[80,320]{1,0:T(8,128)(2,1)S(1)} %slice.3), channel_id=1, source_target_pairs={{0,192},{64,0},{128,64},{192,128},{1,193},{65,1},{129,65},{193,129... | collective-permute-start | bytes 153608 | tf_op jit(solution)/shard_map/ppermute | solution.py:330
  46.5 13.6 %collective-permute-start.6 = (bf16[320,320]{1,0:T(8,128)(2,1)S(1)}, bf16[320,320]{1,0:T(8,128)(2,1)S(1)}, u32[]{:S(2)}, u32[]{:S(2)}) collective-permute-start(bf16[320,320]{1,0:T(8,128)(2,1)S(1)} %pad_maximum_fusion.2.w0_ref), channel_id=1, source_target_pairs={{0,16},{16,32},{32,48},{48,0},{1,17},{17,33},{33,49},{49,1},{2,18}... | collective-permute-start | bytes 614408 | tf_op jit(solution)/shard_map/ppermute | solution.py:330
  49.4 11.6 %collective-permute-start.7 = (bf16[320,320]{1,0:T(8,128)(2,1)S(1)}, bf16[320,320]{1,0:T(8,128)(2,1)S(1)}, u32[]{:S(2)}, u32[]{:S(2)}) collective-permute-start(bf16[320,320]{1,0:T(8,128)(2,1)S(1)} %pad_maximum_fusion.2.w0_ref), channel_id=1, source_target_pairs={{0,32},{16,48},{32,0},{48,16},{1,33},{17,49},{33,1},{49,17},{2,34}... | collective-permute-start | bytes 614408 | tf_op jit(solution)/shard_map/ppermute | solution.py:330
  49.4 14.1 %collective-permute-start.8 = (bf16[320,320]{1,0:T(8,128)(2,1)S(1)}, bf16[320,320]{1,0:T(8,128)(2,1)}, u32[]{:S(2)}, u32[]{:S(2)}) collective-permute-start(bf16[320,320]{1,0:T(8,128)(2,1)S(1)} %pad_maximum_fusion.2.w0_ref), channel_id=1, source_target_pairs={{0,48},{16,0},{32,16},{48,32},{1,49},{17,1},{33,17},{49,33},{2,50}... | collective-permute-start | bytes 614408 | tf_op jit(solution)/shard_map/ppermute | solution.py:330
  63.5 3.0 %collective-permute-start.9 = (bf16[512,1280]{1,0:T(8,128)(2,1)S(1)}, bf16[512,1280]{1,0:T(8,128)(2,1)S(1)}, u32[]{:S(2)}, u32[]{:S(2)}) collective-permute-start(bf16[512,1280]{1,0:T(8,128)(2,1)S(1)} %bitcast.27), channel_id=1, source_target_pairs={{0,1},{1,0},{2,3},{3,2},{4,5},{5,4},{6,7},{7,6},{8,9},{9,8},{10,11... | collective-permute-start | bytes 3932168 | tf_op jit(solution)/shard_map/ppermute | solution.py:369
  80.0 25.8 %all-to-all-start.1 = ((bf16[4,4,80,640]{3,2,1,0:T(8,128)(2,1)}), bf16[4,4,80,640]{3,2,1,0:T(8,128)(2,1)}, u32[]{:S(2)}, u32[]{:S(2)}) async-start(bf16[4,4,80,640]{3,2,1,0:T(8,128)(2,1)} %get-tuple-element.75), calls=%async_computation.1 | async-start | bytes 3276800 | tf_op jit(solution)/shard_map/all_to_all | solution.py:396
  85.2 13.2 %collective-permute-start.10 = (bf16[4,80,640]{2,1,0:T(8,128)(2,1)S(1)}, bf16[4,80,640]{2,1,0:T(8,128)(2,1)S(1)}, u32[]{:S(2)}, u32[]{:S(2)}) collective-permute-start(bf16[4,80,640]{2,1,0:T(8,128)(2,1)S(1)} %copy-done.10), channel_id=1, source_target_pairs={{0,64},{64,128},{128,192},{192,0},{1,65},{65,129},{129,193},{193,1... | collective-permute-start | bytes 1228808 | tf_op jit(solution)/shard_map/ppermute | solution.py:330
  86.8 23.5 %collective-permute-start.13 = (bf16[4,80,640]{2,1,0:T(8,128)(2,1)}, bf16[4,80,640]{2,1,0:T(8,128)(2,1)S(1)}, u32[]{:S(2)}, u32[]{:S(2)}) collective-permute-start(bf16[4,80,640]{2,1,0:T(8,128)(2,1)} %get-tuple-element.73), channel_id=1, source_target_pairs={{0,128},{64,192},{128,0},{192,64},{1,129},{65,193},{129,1},{193,65... | collective-permute-start | bytes 1228808 | tf_op jit(solution)/shard_map/ppermute | solution.py:330
  89.5 20.8 %collective-permute-start.14 = (bf16[4,80,640]{2,1,0:T(8,128)(2,1)}, bf16[4,80,640]{2,1,0:T(8,128)(2,1)}, u32[]{:S(2)}, u32[]{:S(2)}) collective-permute-start(bf16[4,80,640]{2,1,0:T(8,128)(2,1)} %get-tuple-element.74), channel_id=1, source_target_pairs={{0,192},{64,0},{128,64},{192,128},{1,193},{65,1},{129,65},{193,129... | collective-permute-start | bytes 1228808 | tf_op jit(solution)/shard_map/ppermute | solution.py:330
  98.5 9.8 %collective-permute-start.11 = (bf16[528,384]{1,0:T(8,128)(2,1)}, bf16[528,384]{1,0:T(8,128)(2,1)S(1)}, u32[]{:S(2)}, u32[]{:S(2)}) collective-permute-start(bf16[528,384]{1,0:T(8,128)(2,1)} %get-tuple-element.70), channel_id=1, source_target_pairs={{0,1},{1,0},{2,3},{3,2},{4,5},{5,4},{6,7},{7,6},{8,9},{9,8},{10,11... | collective-permute-start | bytes 1216520 | tf_op jit(solution)/shard_map/ppermute | solution.py:413
  98.8 9.5 %collective-permute-start.12 = (bf16[528,384]{1,0:T(8,128)(2,1)}, bf16[528,384]{1,0:T(8,128)(2,1)S(1)}, u32[]{:S(2)}, u32[]{:S(2)}) collective-permute-start(bf16[528,384]{1,0:T(8,128)(2,1)} %get-tuple-element.71), channel_id=1, source_target_pairs={{0,1},{1,0},{2,3},{3,2},{4,5},{5,4},{6,7},{7,6},{8,9},{9,8},{10,11... | collective-permute-start | bytes 1216520 | tf_op jit(solution)/shard_map/ppermute | solution.py:413
  110.3 22.4 %copy-start.14 = (bf16[80,640]{1,0:T(8,128)(2,1)S(1)}, bf16[80,640]{1,0:T(8,128)(2,1)}, u32[]{:S(2)}) copy-start(bf16[80,640]{1,0:T(8,128)(2,1)} %get-tuple-element.85) | copy-start | bytes 307204
  110.3 25.5 %copy-start.13 = (bf16[80,640]{1,0:T(8,128)(2,1)S(1)}, bf16[80,640]{1,0:T(8,128)(2,1)}, u32[]{:S(2)}) copy-start(bf16[80,640]{1,0:T(8,128)(2,1)} %get-tuple-element.86) | copy-start | bytes 307204
  110.3 31.6 %copy-start.2 = (f32[80,640]{1,0:T(8,128)S(1)}, f32[80,640]{1,0:T(8,128)}, u32[]{:S(2)}) copy-start(f32[80,640]{1,0:T(8,128)} %get-tuple-element.83.refs_0_) | copy-start | bytes 614404
  110.3 41.3 %all-to-all-start.2 = ((bf16[128,8,384]{2,1,0:T(8,128)(2,1)}), bf16[128,8,384]{2,1,0:T(8,128)(2,1)S(1)}, u32[]{:S(2)}, u32[]{:S(2)}) async-start(bf16[128,8,384]{2,1,0:T(8,128)(2,1)} %bitcast.18), calls=%async_computation.2 | async-start | bytes 1572864 | tf_op jit(solution)/shard_map/all_to_all | solution.py:419
  123.5 28.1 %copy-start.1 = (f32[512,384]{1,0:T(8,128)S(1)}, f32[512,384]{1,0:T(8,128)}, u32[]{:S(2)}) copy-start(f32[512,384]{1,0:T(8,128)} %shard_map.113.xh_ref) | copy-start | bytes 2359300
  126.1 9.6 %collective-permute-start.18 = (bf16[80,640]{1,0:T(8,128)(2,1)}, bf16[80,640]{1,0:T(8,128)(2,1)S(1)}, u32[]{:S(2)}, u32[]{:S(2)}) collective-permute-start(bf16[80,640]{1,0:T(8,128)(2,1)} %get-tuple-element.92), channel_id=1, source_target_pairs={{0,16},{16,32},{32,48},{48,0},{1,17},{17,33},{33,49},{49,1},{2,18}... | collective-permute-start | bytes 307208 | tf_op jit(solution)/shard_map/ppermute | solution.py:330
  127.7 9.3 %collective-permute-start.19 = (bf16[80,640]{1,0:T(8,128)(2,1)}, bf16[80,640]{1,0:T(8,128)(2,1)S(1)}, u32[]{:S(2)}, u32[]{:S(2)}) collective-permute-start(bf16[80,640]{1,0:T(8,128)(2,1)} %get-tuple-element.93), channel_id=1, source_target_pairs={{0,32},{16,48},{32,0},{48,16},{1,33},{17,49},{33,1},{49,17},{2,34}... | collective-permute-start | bytes 307208 | tf_op jit(solution)/shard_map/ppermute | solution.py:330
  129.1 9.1 %collective-permute-start.20 = (bf16[80,640]{1,0:T(8,128)(2,1)}, bf16[80,640]{1,0:T(8,128)(2,1)S(1)}, u32[]{:S(2)}, u32[]{:S(2)}) collective-permute-start(bf16[80,640]{1,0:T(8,128)(2,1)} %get-tuple-element.94), channel_id=1, source_target_pairs={{0,48},{16,0},{32,16},{48,32},{1,49},{17,1},{33,17},{49,33},{2,50}... | collective-permute-start | bytes 307208 | tf_op jit(solution)/shard_map/ppermute | solution.py:330
  130.9 8.6 %collective-permute-start.15 = (bf16[80,640]{1,0:T(8,128)(2,1)S(1)}, bf16[80,640]{1,0:T(8,128)(2,1)S(1)}, u32[]{:S(2)}, u32[]{:S(2)}) collective-permute-start(bf16[80,640]{1,0:T(8,128)(2,1)S(1)} %copy-done.15), channel_id=1, source_target_pairs={{0,64},{64,128},{128,192},{192,0},{1,65},{65,129},{129,193},{193,1... | collective-permute-start | bytes 307208 | tf_op jit(solution)/shard_map/ppermute | solution.py:330
  132.6 9.2 %collective-permute-start.16 = (bf16[80,640]{1,0:T(8,128)(2,1)S(1)}, bf16[80,640]{1,0:T(8,128)(2,1)S(1)}, u32[]{:S(2)}, u32[]{:S(2)}) collective-permute-start(bf16[80,640]{1,0:T(8,128)(2,1)S(1)} %copy-done.14), channel_id=1, source_target_pairs={{0,128},{64,192},{128,0},{192,64},{1,129},{65,193},{129,1},{193,65... | collective-permute-start | bytes 307208 | tf_op jit(solution)/shard_map/ppermute | solution.py:330
  135.7 6.1 %collective-permute-start.17 = (bf16[80,640]{1,0:T(8,128)(2,1)S(1)}, bf16[80,640]{1,0:T(8,128)(2,1)S(1)}, u32[]{:S(2)}, u32[]{:S(2)}) collective-permute-start(bf16[80,640]{1,0:T(8,128)(2,1)S(1)} %copy-done.13), channel_id=1, source_target_pairs={{0,192},{64,0},{128,64},{192,128},{1,193},{65,1},{129,65},{193,129... | collective-permute-start | bytes 307208 | tf_op jit(solution)/shard_map/ppermute | solution.py:330
  142.9 6.1 %collective-permute-start.21 = (bf16[20,1280]{1,0:T(8,128)(2,1)S(1)}, bf16[20,1280]{1,0:T(8,128)(2,1)S(1)}, u32[]{:S(2)}, u32[]{:S(2)}) collective-permute-start(bf16[20,1280]{1,0:T(8,128)(2,1)S(1)} %get-tuple-element.96), channel_id=1, source_target_pairs={{0,4},{4,8},{8,12},{12,0},{1,5},{5,9},{9,13},{13,1},{2,6},{6,10},{... | collective-permute-start | bytes 153608 | tf_op jit(solution)/shard_map/ppermute | solution.py:330
  144.6 5.1 %collective-permute-start.22 = (bf16[20,1280]{1,0:T(8,128)(2,1)S(1)}, bf16[20,1280]{1,0:T(8,128)(2,1)S(1)}, u32[]{:S(2)}, u32[]{:S(2)}) collective-permute-start(bf16[20,1280]{1,0:T(8,128)(2,1)S(1)} %get-tuple-element.97), channel_id=1, source_target_pairs={{0,8},{4,12},{8,0},{12,4},{1,9},{5,13},{9,1},{13,5},{2,10},{6,14},... | collective-permute-start | bytes 153608 | tf_op jit(solution)/shard_map/ppermute | solution.py:330
  146.6 4.2 %collective-permute-start.23 = (bf16[20,1280]{1,0:T(8,128)(2,1)S(1)}, bf16[20,1280]{1,0:T(8,128)(2,1)S(1)}, u32[]{:S(2)}, u32[]{:S(2)}) collective-permute-start(bf16[20,1280]{1,0:T(8,128)(2,1)S(1)} %get-tuple-element.98), channel_id=1, source_target_pairs={{0,12},{4,0},{8,4},{12,8},{1,13},{5,1},{9,5},{13,9},{2,14},{6,2},{... | collective-permute-start | bytes 153608 | tf_op jit(solution)/shard_map/ppermute | solution.py:330
  (12 other events, 95.7 us)
Sparse Core Ops, SparseCore 0:
  20.8 65.1 all-gather.2
